TPU v7x, 32 devices: a whole 2x2x4 slice. The times are simulated.
32 devices in a mesh: section: 4 (over y, x), dp: 8 (over z, core).
Axes of the slice: x: 2, y: 2, z: 4, core: 2. Of those that a mesh axis runs over, the one named last changes fastest.
Arguments:
- inputs: bfloat16 [2, 1024, 768], P(None, 'dp', 'section'), may hold values from -6 to 6
- cotangent: bfloat16 [2, 1024, 768], P(None, 'dp', 'section'), may hold values from -6 to 6
- seq_lengths: int32 [2], replicated, may hold values from 256 to 1024, as said below
- decay_rates: float32 [4, 768], P('section'), may hold values from 0.5 to 12
- norm_gain: float32 [4, 768], P('section'), may hold values from 0.5 to 1.5
- norm_bias: float32 [4, 768], P('section'), may hold values from -1.25 to 1.25
- in_weight: bfloat16 [4, 768, 2304], P('section'), may hold values from -0.21875 to 0.21875
- in_bias: float32 [4, 2304], P('section'), may hold values from -1.75 to 1.75
- short_weight: float32 [4, 3, 2304], P('section'), may hold values from -3.5 to 3.5
- short_bias: float32 [4, 2304], P('section'), may hold values from -1.75 to 1.75
- filter_weight_one: float32 [4, 33, 64], P('section'), may hold values from -1 to 1
- filter_bias_one: float32 [4, 64], P('section'), may hold values from -6 to 6
- filter_weight_two: float32 [4, 64, 64], P('section'), may hold values from -0.75 to 0.75
- filter_bias_two: float32 [4, 64], P('section'), may hold values from -6 to 6
- filter_weight_out: float32 [4, 64, 768], P('section'), may hold values from -0.0234375 to 0.0234375
- filter_bias_out: float32 [4, 768], P('section'), may hold values from -0.1875 to 0.1875
- skip_gain: float32 [4, 768], P('section'), may hold values from -6 to 6
- out_weight: bfloat16 [4, 768, 768], P('section'), may hold values from -0.21875 to 0.21875
- out_bias: float32 [4, 768], P('section'), may hold values from -1.75 to 1.75
- second_norm_gain: float32 [4, 768], P('section'), may hold values from 0.5 to 1.5
- second_norm_bias: float32 [4, 768], P('section'), may hold values from -1.25 to 1.25
- up_weight: bfloat16 [4, 768, 3072], P('section'), may hold values from -0.21875 to 0.21875
- up_bias: float32 [4, 3072], P('section'), may hold values from -1.75 to 1.75
- down_weight: bfloat16 [4, 3072, 768], P('section'), may hold values from -0.109375 to 0.109375
- down_bias: float32 [4, 768], P('section'), may hold values from -1.75 to 1.75
Outputs:
- outputs: bfloat16 [2, 1024, 768], P(None, 'dp', 'section')
- input_grad: float32 [2, 1024, 768], P(None, 'dp', 'section')
- norm_gain_grad: float32 [4, 768], P('section', 'dp')
- norm_bias_grad: float32 [4, 768], P('section', 'dp')
- in_weight_grad: float32 [4, 768, 2304], P('section', 'dp')
- in_bias_grad: float32 [4, 2304], P('section', 'dp')
- short_weight_grad: float32 [4, 3, 2304], P('section', None, 'dp')
- short_bias_grad: float32 [4, 2304], P('section', 'dp')
- filter_weight_one_grad: float32 [4, 33, 64], P('section', None, 'dp')
- filter_bias_one_grad: float32 [4, 64], P('section', 'dp')
- filter_weight_two_grad: float32 [4, 64, 64], P('section', 'dp')
- filter_bias_two_grad: float32 [4, 64], P('section', 'dp')
- filter_weight_out_grad: float32 [4, 64, 768], P('section', 'dp')
- filter_bias_out_grad: float32 [4, 768], P('section', 'dp')
- skip_gain_grad: float32 [4, 768], P('section', 'dp')
- out_weight_grad: float32 [4, 768, 768], P('section', 'dp')
- out_bias_grad: float32 [4, 768], P('section', 'dp')
- second_norm_gain_grad: float32 [4, 768], P('section', 'dp')
- second_norm_bias_grad: float32 [4, 768], P('section', 'dp')
- up_weight_grad: float32 [4, 768, 3072], P('section', 'dp')
- up_bias_grad: float32 [4, 3072], P('section', 'dp')
- down_weight_grad: float32 [4, 3072, 768], P('section', 'dp')
- down_bias_grad: float32 [4, 768], P('section', 'dp')
Inputs may be any that keep to these rules, and one draw needn't show every extreme that they name: micro-batch m has seq_lengths[m] live positions at its start and padding after them; one micro-batch, drawn from the seed, has all 1024.
All inputs are finite; a program needn't handle non-finite values.
Results may differ from a plain program's by a relative error of at most 0.039.
Values may be sent and summed in bfloat16 or wider, within the bound.
A program may use at most 256 MiB of HBM per device.

v0:
```python
import jax
import jax.numpy as jnp
from jax import lax
from jax.sharding import PartitionSpec as P

EMB = 33


norm_epsilon = 1e-05
sine_scale = 14.0
highest = lax.Precision.HIGHEST


def as_sent(value):
    return jax.tree.map(lambda a: a.astype(jnp.bfloat16) if a.dtype == jnp.float32 else a, value)


def from_behind(value, axis, by):
    count = lax.axis_size(axis)
    pairs = [(i, i + by) for i in range(count) if 0 <= i + by < count]
    return lax.ppermute(value, axis, pairs)


def layer_norm(signal, factor, offset):
    centred = signal - jnp.mean(signal, axis=-1, keepdims=True)
    spread = jnp.mean(centred * centred, axis=-1, keepdims=True)
    return centred * lax.rsqrt(spread + norm_epsilon) * factor + offset


def exact_product(former, latter):
    return jnp.dot(former, latter, precision=highest, preferred_element_type=jnp.float32)


def low_product(former, latter):
    return jnp.dot(former, latter, preferred_element_type=jnp.float32)


def rows_product(former, latter):
    return lax.dot_general(
        former, latter, (((0,), (0,)), ((), ())), preferred_element_type=jnp.float32
    )


def back_product(former, latter):
    return lax.dot_general(
        former, latter, (((1,), (1,)), ((), ())), preferred_element_type=jnp.float32
    )


def exact_einsum(pattern, former, latter):
    return jnp.einsum(pattern, former, latter, precision=highest)


def turn_table(numerator, period):
    angles = 2.0 * jnp.pi * numerator.astype(jnp.float32) / period
    return (jnp.cos(angles), jnp.sin(angles))


def position_features(positions, length_total):
    scaled = positions.astype(jnp.float32) / length_total
    frequency = jnp.arange(1, (EMB - 1) // 2 + 1)
    turn_counts = positions[:, None] * frequency[None, :] % length_total
    angles = 2.0 * jnp.pi * turn_counts.astype(jnp.float32) / length_total
    return (jnp.concatenate([scaled[:, None], jnp.cos(angles), jnp.sin(angles)], axis=1), scaled)


def filter_values(
    first_weight,
    first_bias,
    second_weight,
    second_bias,
    third_weight,
    third_bias,
    decay_rate,
    features,
    scaled,
):
    layer_one = jnp.sin(sine_scale * (exact_product(features, first_weight) + first_bias))
    layer_two = jnp.sin(sine_scale * (exact_product(layer_one, second_weight) + second_bias))
    raw_kernel = exact_product(layer_two, third_weight) + third_bias
    return raw_kernel * jnp.exp(-decay_rate[None, :] * scaled[:, None])


def forward_transform(signal):
    part_count = lax.axis_size("dp")
    dp_index = lax.axis_index("dp")
    row_count = signal.shape[0]
    block_rows = row_count // part_count
    transform_size = 2 * part_count * row_count
    spread_rows = lax.all_to_all(
        signal.reshape(part_count, block_rows, -1).astype(jnp.bfloat16),
        "dp",
        split_axis=0,
        concat_axis=0,
        tiled=True,
    ).astype(jnp.float32)
    coarse = jnp.arange(2 * part_count)
    coarse_cos, coarse_sin = turn_table(
        coarse[:, None] * jnp.arange(part_count)[None, :] % (2 * part_count), 2 * part_count
    )
    real_first = exact_einsum("kp,pmc->kmc", coarse_cos, spread_rows)
    imag_first = -exact_einsum("kp,pmc->kmc", coarse_sin, spread_rows)
    offsets = dp_index * block_rows + jnp.arange(block_rows)
    twist_cos, twist_sin = turn_table(
        coarse[:, None] * offsets[None, :] % transform_size, transform_size
    )
    twist_cos = twist_cos[:, :, None]
    twist_sin = twist_sin[:, :, None]
    real_twist = real_first * twist_cos + imag_first * twist_sin
    imag_twist = imag_first * twist_cos - real_first * twist_sin
    real_group, imag_group = (
        lax.all_to_all(as_sent(real_twist), "dp", split_axis=0, concat_axis=1, tiled=True).astype(
            real_twist.dtype
        ),
        lax.all_to_all(as_sent(imag_twist), "dp", split_axis=0, concat_axis=1, tiled=True).astype(
            imag_twist.dtype
        ),
    )
    fine_index = jnp.arange(row_count)
    fine_cos, fine_sin = turn_table(
        fine_index[:, None] * fine_index[None, :] % row_count, row_count
    )
    real_out = exact_einsum("km,jmc->jkc", fine_cos, real_group) + exact_einsum(
        "km,jmc->jkc", fine_sin, imag_group
    )
    imag_out = exact_einsum("km,jmc->jkc", fine_cos, imag_group) - exact_einsum(
        "km,jmc->jkc", fine_sin, real_group
    )
    return (real_out, imag_out)


def inverse_transform(real_part, imag_part):
    part_count = lax.axis_size("dp")
    dp_index = lax.axis_index("dp")
    row_count = real_part.shape[1]
    transform_size = 2 * part_count * row_count
    fine_index = jnp.arange(row_count)
    fine_cos, fine_sin = turn_table(
        fine_index[:, None] * fine_index[None, :] % row_count, row_count
    )
    real_first = exact_einsum("mk,jkc->jmc", fine_cos, real_part) - exact_einsum(
        "mk,jkc->jmc", fine_sin, imag_part
    )
    imag_first = exact_einsum("mk,jkc->jmc", fine_cos, imag_part) + exact_einsum(
        "mk,jkc->jmc", fine_sin, real_part
    )
    coarse_local = 2 * dp_index + jnp.arange(2)
    twist_cos, twist_sin = turn_table(
        coarse_local[:, None] * fine_index[None, :] % transform_size, transform_size
    )
    twist_cos = twist_cos[:, :, None]
    twist_sin = twist_sin[:, :, None]
    real_twist = real_first * twist_cos - imag_first * twist_sin
    imag_twist = imag_first * twist_cos + real_first * twist_sin
    real_group, imag_group = (
        lax.all_to_all(as_sent(real_twist), "dp", split_axis=1, concat_axis=0, tiled=True).astype(
            real_twist.dtype
        ),
        lax.all_to_all(as_sent(imag_twist), "dp", split_axis=1, concat_axis=0, tiled=True).astype(
            imag_twist.dtype
        ),
    )
    coarse = jnp.arange(2 * part_count)
    coarse_cos, coarse_sin = turn_table(
        jnp.arange(part_count)[:, None] * coarse[None, :] % (2 * part_count), 2 * part_count
    )
    values = (
        exact_einsum("pk,kmc->pmc", coarse_cos, real_group)
        - exact_einsum("pk,kmc->pmc", coarse_sin, imag_group)
    ) / transform_size
    returned = lax.all_to_all(
        as_sent(values), "dp", split_axis=0, concat_axis=1, tiled=True
    ).astype(values.dtype)
    return returned.reshape(row_count, -1)


def spectral_product(former, latter, conjugate):
    former_real, former_imag = former
    latter_real, latter_imag = latter
    if conjugate:
        former_imag = -former_imag
    return (
        former_real * latter_real - former_imag * latter_imag,
        former_real * latter_imag + former_imag * latter_real,
    )


def block_forward(weights, spectrum, hidden_state):
    (
        norm_gain,
        norm_bias,
        in_weight,
        in_bias,
        short_weight,
        short_bias,
        filter_weight_one,
        filter_bias_one,
        filter_weight_two,
        filter_bias_two,
        filter_weight_out,
        filter_bias_out,
        skip_gain,
        out_weight,
        out_bias,
        second_norm_gain,
        second_norm_bias,
        up_weight,
        up_bias,
        down_weight,
        down_bias,
    ) = weights
    model_width = norm_gain.shape[0]
    normed = layer_norm(hidden_state, norm_gain, norm_bias).astype(jnp.bfloat16)
    mixed_rows = low_product(normed, in_weight) + in_bias
    before = from_behind(mixed_rows[-2:], "dp", 1)
    padded = jnp.concatenate([before, mixed_rows], axis=0)
    short_out = (
        short_weight[0] * mixed_rows
        + short_weight[1] * padded[1:-1]
        + short_weight[2] * padded[:-2]
        + short_bias
    )
    gate_out = short_out[:, :model_width]
    gate_in = short_out[:, model_width : 2 * model_width]
    value = short_out[:, 2 * model_width :]
    middle = gate_in * value
    spectrum_mid = forward_transform(middle)
    conv_out = (
        inverse_transform(*spectral_product(spectrum_mid, spectrum, False)) + skip_gain * middle
    )
    gated_out = (gate_out * conv_out).astype(jnp.bfloat16)
    residual = hidden_state + (low_product(gated_out, out_weight) + out_bias)
    normed_two = layer_norm(residual, second_norm_gain, second_norm_bias).astype(jnp.bfloat16)
    hidden = low_product(normed_two, up_weight) + up_bias
    active = jax.nn.gelu(hidden).astype(jnp.bfloat16)
    output = (residual + (low_product(active, down_weight) + down_bias)).astype(jnp.bfloat16)
    stashed = (
        hidden_state,
        normed,
        mixed_rows,
        before,
        short_out,
        middle,
        spectrum_mid,
        conv_out,
        gated_out,
        residual,
        normed_two,
        hidden,
        active,
    )
    kept = (hidden_state, before, short_out, middle, spectrum_mid, conv_out, gated_out)
    return (output, stashed, kept)


def block_backward(weights, spectrum, stashed, grad_out):
    (
        norm_gain,
        norm_bias,
        in_weight,
        in_bias,
        short_weight,
        short_bias,
        filter_weight_one,
        filter_bias_one,
        filter_weight_two,
        filter_bias_two,
        filter_weight_out,
        filter_bias_out,
        skip_gain,
        out_weight,
        out_bias,
        second_norm_gain,
        second_norm_bias,
        up_weight,
        up_bias,
        down_weight,
        down_bias,
    ) = weights
    (
        hidden_state,
        normed,
        mixed_rows,
        before,
        short_out,
        middle,
        spectrum_mid,
        conv_out,
        gated_out,
        residual,
        normed_two,
        hidden,
        active,
    ) = stashed
    model_width = norm_gain.shape[0]
    gate_out = short_out[:, :model_width]
    gate_in = short_out[:, model_width : 2 * model_width]
    value = short_out[:, 2 * model_width :]
    grad_low = grad_out.astype(jnp.bfloat16)
    down_grad = rows_product(active, grad_low)
    down_bias_grad = jnp.sum(grad_low.astype(jnp.float32), axis=0)
    grad_active = back_product(grad_low, down_weight)
    _, gelu_pullback = jax.vjp(jax.nn.gelu, hidden)
    grad_hidden = gelu_pullback(grad_active)[0].astype(jnp.bfloat16)
    up_grad = rows_product(normed_two, grad_hidden)
    up_bias_grad = jnp.sum(grad_hidden.astype(jnp.float32), axis=0)
    _, second_pullback = jax.vjp(layer_norm, residual, second_norm_gain, second_norm_bias)
    grad_norm_res, second_gain_grad, second_bias_grad = second_pullback(
        back_product(grad_hidden, up_weight)
    )
    grad_residual = grad_low.astype(jnp.float32) + grad_norm_res
    grad_branch = grad_residual.astype(jnp.bfloat16)
    out_grad = rows_product(gated_out, grad_branch)
    out_bias_grad = jnp.sum(grad_branch.astype(jnp.float32), axis=0)
    grad_gated = back_product(grad_branch, out_weight)
    grad_conv = grad_gated * gate_out
    grad_gate_out = grad_gated * conv_out
    skip_grad = jnp.sum(grad_conv * middle, axis=0)
    grad_spectrum = forward_transform(grad_conv)
    grad_middle = skip_gain * grad_conv + inverse_transform(
        *spectral_product(spectrum, grad_spectrum, True)
    )
    kernel_grad = spectral_product(spectrum_mid, grad_spectrum, True)
    grad_gate_in = grad_middle * value
    grad_value = grad_middle * gate_in
    grad_short = jnp.concatenate([grad_gate_out, grad_gate_in, grad_value], axis=1)
    after_rows = from_behind(grad_short[:2], "dp", -1)
    extended = jnp.concatenate([grad_short, after_rows], axis=0)
    padded = jnp.concatenate([before, mixed_rows], axis=0)
    short_grad = jnp.stack(
        [
            jnp.sum(grad_short * mixed_rows, axis=0),
            jnp.sum(grad_short * padded[1:-1], axis=0),
            jnp.sum(grad_short * padded[:-2], axis=0),
        ]
    )
    short_bias_grad = jnp.sum(grad_short, axis=0)
    grad_mixed = (
        short_weight[0] * grad_short
        + short_weight[1] * extended[1:-1]
        + short_weight[2] * extended[2:]
    ).astype(jnp.bfloat16)
    in_grad = rows_product(normed, grad_mixed)
    in_bias_grad = jnp.sum(grad_mixed.astype(jnp.float32), axis=0)
    _, first_pullback = jax.vjp(layer_norm, hidden_state, norm_gain, norm_bias)
    grad_norm_in, gain_grad, bias_grad = first_pullback(back_product(grad_mixed, in_weight))
    grad_state = grad_residual + grad_norm_in
    grads = (
        gain_grad,
        bias_grad,
        in_grad,
        in_bias_grad,
        short_grad,
        short_bias_grad,
        skip_grad,
        out_grad,
        out_bias_grad,
        second_gain_grad,
        second_bias_grad,
        up_grad,
        up_bias_grad,
        down_grad,
        down_bias_grad,
    )
    return (grad_state, grads, kernel_grad)


def local(
    inputs,
    cotangent,
    seq_lengths,
    decay_rates,
    norm_gain,
    norm_bias,
    in_weight,
    in_bias,
    short_weight,
    short_bias,
    filter_weight_one,
    filter_bias_one,
    filter_weight_two,
    filter_bias_two,
    filter_weight_out,
    filter_bias_out,
    skip_gain,
    out_weight,
    out_bias,
    second_norm_gain,
    second_norm_bias,
    up_weight,
    up_bias,
    down_weight,
    down_bias,
):
    sections = lax.axis_size("section")
    section_index = lax.axis_index("section")
    part_count = lax.axis_size("dp")
    dp_index = lax.axis_index("dp")
    whole_in, whole_grad = (
        lax.all_gather(inputs, "section", axis=2, tiled=True),
        lax.all_gather(cotangent, "section", axis=2, tiled=True),
    )
    micro_count, row_count, model_width = whole_in.shape
    weights = tuple(
        (
            tensor[0]
            for tensor in (
                norm_gain,
                norm_bias,
                in_weight,
                in_bias,
                short_weight,
                short_bias,
                filter_weight_one,
                filter_bias_one,
                filter_weight_two,
                filter_bias_two,
                filter_weight_out,
                filter_bias_out,
                skip_gain,
                out_weight,
                out_bias,
                second_norm_gain,
                second_norm_bias,
                up_weight,
                up_bias,
                down_weight,
                down_bias,
            )
        )
    )
    decay_rate = decay_rates[0]
    positions = dp_index * row_count + jnp.arange(row_count)
    features, scaled = position_features(positions, part_count * row_count)
    live_rows = (positions[None, :] < seq_lengths[:, None]).astype(jnp.float32)
    tick_count = micro_count + sections - 1
    fixed_spectrum = forward_transform(filter_values(*weights[6:12], decay_rate, features, scaled))

    def forward_tick(incoming, tick_index):
        slot_index = jnp.clip(tick_index - section_index, 0, micro_count - 1)
        hidden_state = jnp.where(section_index == 0, whole_in[slot_index], incoming).astype(
            jnp.float32
        )
        output, stashed, kept = block_forward(weights, fixed_spectrum, hidden_state)
        passed = from_behind(output, "section", 1)
        return (passed, (output, stashed))

    start_rows = jnp.zeros((row_count, model_width), jnp.bfloat16)
    _, (outputs_all, stash) = lax.scan(forward_tick, start_rows, jnp.arange(tick_count))
    chosen = (0, 1, 2, 3, 4, 5, 12, 13, 14, 15, 16, 17, 18, 19, 20)
    start_totals = tuple((jnp.zeros(weights[position].shape, jnp.float32) for position in chosen))
    kernel_zero = jnp.zeros(fixed_spectrum[0].shape, jnp.float32)

    def backward_tick(carry, tick_index):
        incoming, totals, kernel_total = carry
        micro_index = tick_index - (sections - 1 - section_index)
        is_valid = (micro_index >= 0) & (micro_index < micro_count)
        slot_index = jnp.clip(micro_index, 0, micro_count - 1)
        top_grad = whole_grad[slot_index].astype(jnp.float32) * live_rows[slot_index][:, None]
        grad_out = jnp.where(section_index == sections - 1, top_grad, incoming.astype(jnp.float32))
        stashed = jax.tree.map(lambda buffer: buffer[slot_index + section_index], stash)
        grad_state, grads, kernel_grad = block_backward(weights, fixed_spectrum, stashed, grad_out)
        totals = jax.tree.map(
            lambda running, addend: running + jnp.where(is_valid, addend, 0.0), totals, grads
        )
        kernel_total = jax.tree.map(
            lambda running, addend: running + jnp.where(is_valid, addend, 0.0),
            kernel_total,
            kernel_grad,
        )
        passed = from_behind(grad_state.astype(jnp.bfloat16), "section", -1)
        return ((passed, totals, kernel_total), grad_state)

    carry_start = (start_rows, start_totals, (kernel_zero, kernel_zero))
    (_, totals, kernel_total), grads_in = lax.scan(
        backward_tick, carry_start, jnp.arange(tick_count)
    )
    kernel_grad = inverse_transform(*kernel_total)

    def filter_local(weight_one, bias_one, weight_two, bias_two, weight_out, bias_out):
        return filter_values(
            weight_one,
            bias_one,
            weight_two,
            bias_two,
            weight_out,
            bias_out,
            decay_rate,
            features,
            scaled,
        )

    _, filter_pullback = jax.vjp(filter_local, *weights[6:12])
    filter_grads = tuple(filter_pullback(kernel_grad))
    all_grads = totals[:6] + filter_grads + totals[6:]
    summed = (
        lax.psum_scatter(all_grads[0], "dp", scatter_dimension=0, tiled=True),
        lax.psum_scatter(all_grads[1], "dp", scatter_dimension=0, tiled=True),
        lax.psum_scatter(all_grads[2], "dp", scatter_dimension=0, tiled=True),
        lax.psum_scatter(all_grads[3], "dp", scatter_dimension=0, tiled=True),
        lax.psum_scatter(all_grads[4], "dp", scatter_dimension=1, tiled=True),
        lax.psum_scatter(all_grads[5], "dp", scatter_dimension=0, tiled=True),
        lax.psum_scatter(all_grads[6], "dp", scatter_dimension=1, tiled=True),
        lax.psum_scatter(all_grads[7], "dp", scatter_dimension=0, tiled=True),
        lax.psum_scatter(all_grads[8], "dp", scatter_dimension=0, tiled=True),
        lax.psum_scatter(all_grads[9], "dp", scatter_dimension=0, tiled=True),
        lax.psum_scatter(all_grads[10], "dp", scatter_dimension=0, tiled=True),
        lax.psum_scatter(all_grads[11], "dp", scatter_dimension=0, tiled=True),
        lax.psum_scatter(all_grads[12], "dp", scatter_dimension=0, tiled=True),
        lax.psum_scatter(all_grads[13], "dp", scatter_dimension=0, tiled=True),
        lax.psum_scatter(all_grads[14], "dp", scatter_dimension=0, tiled=True),
        lax.psum_scatter(all_grads[15], "dp", scatter_dimension=0, tiled=True),
        lax.psum_scatter(all_grads[16], "dp", scatter_dimension=0, tiled=True),
        lax.psum_scatter(all_grads[17], "dp", scatter_dimension=0, tiled=True),
        lax.psum_scatter(all_grads[18], "dp", scatter_dimension=0, tiled=True),
        lax.psum_scatter(all_grads[19], "dp", scatter_dimension=0, tiled=True),
        lax.psum_scatter(all_grads[20], "dp", scatter_dimension=0, tiled=True),
    )
    final_rows = (
        outputs_all[sections - 1 : sections - 1 + micro_count].astype(jnp.float32)
        * live_rows[:, :, None]
    )
    final_rows = jnp.where(section_index == sections - 1, final_rows, 0.0)
    entry_grad = jnp.where(
        section_index == 0, grads_in[sections - 1 : sections - 1 + micro_count], 0.0
    )
    shown_rows, input_grad = (
        lax.psum_scatter(
            final_rows.astype(jnp.bfloat16), "section", scatter_dimension=2, tiled=True
        ).astype(jnp.float32),
        lax.psum_scatter(
            entry_grad.astype(jnp.bfloat16), "section", scatter_dimension=2, tiled=True
        ).astype(jnp.float32),
    )
    return (shown_rows.astype(jnp.bfloat16), input_grad) + tuple(
        (summed_grad[None] for summed_grad in summed)
    )


def solution(mesh):
    in_specs = (
        P(None, "dp", "section"),
        P(None, "dp", "section"),
        P(),
        P("section", None),
        P("section", None),
        P("section", None),
        P("section", None, None),
        P("section", None),
        P("section", None, None),
        P("section", None),
        P("section", None, None),
        P("section", None),
        P("section", None, None),
        P("section", None),
        P("section", None, None),
        P("section", None),
        P("section", None),
        P("section", None, None),
        P("section", None),
        P("section", None),
        P("section", None),
        P("section", None, None),
        P("section", None),
        P("section", None, None),
        P("section", None),
    )
    out_specs = (
        P(None, "dp", "section"),
        P(None, "dp", "section"),
        P("section", "dp"),
        P("section", "dp"),
        P("section", "dp", None),
        P("section", "dp"),
        P("section", None, "dp"),
        P("section", "dp"),
        P("section", None, "dp"),
        P("section", "dp"),
        P("section", "dp", None),
        P("section", "dp"),
        P("section", "dp", None),
        P("section", "dp"),
        P("section", "dp"),
        P("section", "dp", None),
        P("section", "dp"),
        P("section", "dp"),
        P("section", "dp"),
        P("section", "dp", None),
        P("section", "dp"),
        P("section", "dp", None),
        P("section", "dp"),
    )
    return jax.shard_map(local, mesh=mesh, in_specs=in_specs, out_specs=out_specs, check_vma=False)
```

profile of v0, /device:TPU:0, one launch (start us, length us, event | category | flops | bytes accessed | tf_op | source)
XLA Modules:
  0.0 2084.4 jit_solution(2117173511954990495)
XLA Ops:
  20.6 8.2 all-to-all-done.12
  34.8 9.5 all_gather.6
  46.2 10.0 all_gather.7
  65.0 10.4 all-to-all-done.14
  80.1 685.6 %while.93 = (s32[]{:T(128)}, bf16[128,768]{1,0:T(8,128)(2,1)}, bf16[5,128,768]{1,2,0:T(8,128)(2,1)}, f32[5,128,768]{2,1,0:T(8,128)}, bf16[5,128,768]{2,1,0:T(8,1...) while((s32[]{:T(128)}, bf16[128,768]{1,0:T(8,128)(2,1)}, ...), condition=%wide.region_5.6_spmd, body=%wide.region_0.5_spmd.sunk | while | flops 4325849088 | bytes 108347200 | solution.py:449
  99.9 8.2 all-to-all-done
  114.6 11.6 all-to-all-done.1
  131.3 11.6 all-to-all-done.2
  158.1 11.4 all-to-all-done.3
  236.2 8.2 all-to-all-done
  251.0 11.6 all-to-all-done.1
  267.6 11.6 all-to-all-done.2
  294.5 11.4 all-to-all-done.3
  372.8 8.2 all-to-all-done
  387.6 11.6 all-to-all-done.1
  404.3 11.6 all-to-all-done.2
  431.1 11.4 all-to-all-done.3
  510.2 8.2 all-to-all-done
  525.0 11.6 all-to-all-done.1
  541.6 11.6 all-to-all-done.2
  568.4 11.4 all-to-all-done.3
  647.7 8.2 all-to-all-done
  662.5 11.6 all-to-all-done.1
  679.2 11.6 all-to-all-done.2
  706.0 11.4 all-to-all-done.3
  766.4 760.9 %while.94 = (s32[]{:T(128)}, bf16[128,768]{1,0:T(8,128)(2,1)}, f32[768]{0:T(1024)}, f32[768]{0:T(1024)}, f32[768,2304]{1,0:T(8,128)}, /*index=5*/f32[2304]{0:T(1...) while((s32[]{:T(128)}, bf16[128,768]{1,0:T(8,128)(2,1)}, ...), condition=%wide.region_29.30_spmd.clone, body=%wide.region_7.29_spmd.clone.sunk | while | flops 6169510912 | bytes 223633168 | solution.py:475
  808.8 7.9 all-to-all-done.6
  843.9 8.3 all-to-all-done.8
  888.2 7.6 all-to-all-done.10
  956.9 7.9 all-to-all-done.6
  971.9 8.9 select_add_fusion.38
  992.0 8.3 all-to-all-done.8
  1015.5 9.0 select_add_fusion.40
  1036.3 7.6 all-to-all-done.10
  1070.8 7.1 select_add_fusion.30
  1105.6 7.9 all-to-all-done.6
  1120.5 8.9 select_add_fusion.38
  1140.6 8.3 all-to-all-done.8
  1164.2 9.0 select_add_fusion.40
  1185.0 7.6 all-to-all-done.10
  1219.5 7.1 select_add_fusion.30
  1254.8 7.9 all-to-all-done.6
  1269.7 8.9 select_add_fusion.38
  1289.9 8.3 all-to-all-done.8
  1313.4 9.0 select_add_fusion.40
  1334.2 7.6 all-to-all-done.10
  1368.7 7.1 select_add_fusion.30
  1404.0 7.9 all-to-all-done.6
  1419.0 8.9 select_add_fusion.38
  1439.1 8.3 all-to-all-done.8
  1462.6 9.0 select_add_fusion.40
  1483.4 7.6 all-to-all-done.10
  1517.9 7.1 select_add_fusion.30
  1538.5 11.4 all-to-all-done.15
  1554.3 11.5 all-to-all-done.16
  1592.8 19.7 reduce-scatter.25.cloned.1.call-done
  1614.1 24.0 %reduce-scatter.13.cloned.1.call-done = bf16[2,128,192]{1,2,0:T(8,128)(2,1)} async-done(((bf16[2,128,768]{1,2,0:T(8,128)(2,1)}), bf16[2,128,192]{1,2,0:T(8,128)(2,1)}) %reduce-scatter.13.cloned.1.call-update) | async-done | bytes 98320 | tf_op jit(solution)/shard_map/reduce_scatter | solution.py:531
  1639.7 56.8 %all-reduce.18.cloned.1.call-done = (f32[768]{0:T(1024)}, f32[768]{0:T(1024)}, f32[2304]{0:T(1024)}, f32[2304]{0:T(1024)}, f32[33,64]{0,1:T(8,128)}, /*index=5*/...) async-done(((f32[768]{0:T(1024)}, f32[768]{0:T(1024)}, ...) | async-done | bytes 80656
  1709.5 16.8 reduce-scatter.11.cloned.1.call-done
  1726.2 33.1 %reduce-scatter.17.cloned.1.call-done = f32[8,768]{1,0:T(8,128)} async-done(((f32[64,768]{1,0:T(8,128)}), f32[8,768]{1,0:T(8,128)}) %reduce-scatter.17.cloned.1.call-update) | async-done | bytes 24592 | tf_op jit(solution)/shard_map/reduce_scatter | solution.py:507
  1759.3 37.2 %reduce-scatter.19.cloned.1.call-done = f32[96,768]{1,0:T(8,128)} async-done(((f32[768,768]{1,0:T(8,128)}), f32[96,768]{1,0:T(8,128)}) %reduce-scatter.19.cloned.1.call-update) | async-done | bytes 294928 | tf_op jit(solution)/shard_map/reduce_scatter | solution.py:510
  1796.5 79.4 %reduce-scatter.15.cloned.1.call-done = f32[96,2304]{1,0:T(8,128)} async-done(((f32[768,2304]{1,0:T(8,128)}), f32[96,2304]{1,0:T(8,128)}) %reduce-scatter.15.cloned.1.call-update) | async-done | bytes 884752 | tf_op jit(solution)/shard_map/reduce_scatter | solution.py:499
  1875.9 100.8 %reduce-scatter.21.cloned.1.call-done = f32[96,3072]{1,0:T(8,128)} async-done(((f32[768,3072]{1,0:T(8,128)}), f32[96,3072]{1,0:T(8,128)}) %reduce-scatter.21.cloned.1.call-update) | async-done | bytes 1179664 | tf_op jit(solution)/shard_map/reduce_scatter | solution.py:514
  1976.7 100.8 %reduce-scatter.23.cloned.1.call-done = f32[384,768]{1,0:T(8,128)} async-done(((f32[3072,768]{1,0:T(8,128)}), f32[384,768]{1,0:T(8,128)}) %reduce-scatter.23.cloned.1.call-update) | async-done | bytes 1179664 | tf_op jit(solution)/shard_map/reduce_scatter | solution.py:516
  (1701 shorter events, 1072.9 us)
Async XLA Ops:
  14.1 14.7 all-to-all-start.12
  30.9 27.2 %all-to-all-start.13 = ((bf16[16,16,768]{2,1,0:T(8,128)(2,1)}), bf16[16,16,768]{2,1,0:T(8,128)(2,1)S(1)}, u32[]{:S(2)}, u32[]{:S(2)}) async-start(bf16[16,16,768]{2,1,0:T(8,128)(2,1)} %copy.202), calls=%async_computation.13 | async-start | bytes 786432 | tf_op jit(solution)/shard_map/all_to_all | solution.py:112
  58.1 17.3 all-to-all-start.14
  95.4 12.7 all-to-all-start
  110.3 15.9 all-to-all-start.1
  126.2 16.6 all-to-all-start.2
  153.5 15.9 all-to-all-start.3
  169.5 15.9 all-to-all-start.4
  187.1 11.7 all-to-all-start.5
  231.5 12.9 all-to-all-start
  246.6 15.9 all-to-all-start.1
  262.6 16.6 all-to-all-start.2
  289.9 15.9 all-to-all-start.3
  305.8 15.9 all-to-all-start.4
  323.5 11.7 all-to-all-start.5
  368.1 12.9 all-to-all-start
  383.3 15.9 all-to-all-start.1
  399.2 16.6 all-to-all-start.2
  426.5 15.9 all-to-all-start.3
  442.5 15.9 all-to-all-start.4
  505.5 12.9 all-to-all-start
  520.6 15.9 all-to-all-start.1
  536.6 16.6 all-to-all-start.2
  563.9 15.9 all-to-all-start.3
  579.8 15.9 all-to-all-start.4
  643.0 12.9 all-to-all-start
  658.2 15.9 all-to-all-start.1
  674.1 16.6 all-to-all-start.2
  701.5 15.9 all-to-all-start.3
  717.4 15.9 all-to-all-start.4
  819.6 16.7 all-to-all-start.7
  836.3 15.9 all-to-all-start.8
  864.0 15.9 all-to-all-start.9
  879.9 15.9 all-to-all-start.10
  953.1 11.7 all-to-all-start.6
  967.7 16.7 all-to-all-start.7
  984.4 15.9 all-to-all-start.8
  1012.1 15.9 all-to-all-start.9
  1028.0 15.9 all-to-all-start.10
  1116.4 16.7 all-to-all-start.7
  1133.1 15.9 all-to-all-start.8
  1160.7 15.9 all-to-all-start.9
  1176.7 15.9 all-to-all-start.10
  1265.6 16.7 all-to-all-start.7
  1282.3 15.9 all-to-all-start.8
  1309.9 15.9 all-to-all-start.9
  1325.9 15.9 all-to-all-start.10
  1343.5 11.7 all-to-all-start.11
  1414.8 16.7 all-to-all-start.7
  1431.5 15.9 all-to-all-start.8
  1459.2 15.9 all-to-all-start.9
  1475.1 15.9 all-to-all-start.10
  1533.9 15.9 all-to-all-start.15
  1549.9 15.9 all-to-all-start.16
  1567.5 11.8 all-to-all-start.17
  1571.0 41.5 %reduce-scatter.25.cloned.1.call-start = ((), (), s32[]{:S(2)}) async-start(), calls=%async_computation.33 | async-start | bytes 1327104
  1572.6 65.5 %reduce-scatter.13.cloned.1.call-start = ((), (), s32[]{:S(2)}) async-start(), calls=%async_computation.27 | async-start | bytes 491520 | tf_op jit(solution)/shard_map/reduce_scatter | solution.py:531
  1574.5 122.0 %all-reduce.18.cloned.1.call-start = ((), (), s32[]{:S(2)}) async-start(), calls=%async_computation.34 | async-start | bytes 272384
  1583.6 142.7 %reduce-scatter.11.cloned.1.call-start = ((), (), s32[]{:S(2)}) async-start(), calls=%async_computation.26 | async-start | bytes 491520 | tf_op jit(solution)/shard_map/reduce_scatter | solution.py:528
  1585.5 173.8 %reduce-scatter.17.cloned.1.call-start = ((), (), s32[]{:S(2)}) async-start(), calls=%async_computation.29 | async-start | bytes 221184 | tf_op jit(solution)/shard_map/reduce_scatter | solution.py:507
  1586.8 209.7 %reduce-scatter.19.cloned.1.call-start = ((), (), s32[]{:S(2)}) async-start(), calls=%async_computation.30 | async-start | bytes 2654208 | tf_op jit(solution)/shard_map/reduce_scatter | solution.py:510
  1587.3 288.6 %reduce-scatter.15.cloned.1.call-start = ((), (), s32[]{:S(2)}) async-start(), calls=%async_computation.28 | async-start | bytes 7962624 | tf_op jit(solution)/shard_map/reduce_scatter | solution.py:499
  1588.1 388.6 %reduce-scatter.21.cloned.1.call-start = ((), (), s32[]{:S(2)}) async-start(), calls=%async_computation.31 | async-start | bytes 10616832 | tf_op jit(solution)/shard_map/reduce_scatter | solution.py:514
  1588.8 488.7 %reduce-scatter.23.cloned.1.call-start = ((), (), s32[]{:S(2)}) async-start(), calls=%async_computation.32 | async-start | bytes 10616832 | tf_op jit(solution)/shard_map/reduce_scatter | solution.py:516
  (377 other events, 2677.1 us)
Sparse Core Ops, SparseCore 0:
  1574.1 38.3 reduce-scatter.24
  1615.3 22.8 reduce-scatter.12
  1642.8 53.6 all-reduce.17
  1700.0 26.1 reduce-scatter.10
  1729.0 30.2 reduce-scatter.16
  1762.1 34.3 reduce-scatter.18
  1799.4 76.4 reduce-scatter.14
  1878.8 97.8 reduce-scatter.20
  1979.6 97.8 reduce-scatter.22
where the time goes:
time: 2100 us; the launch traced here: 2080 us
  waiting for transfers between devices  972 us (46%)
  matrix products  393 us (19%)
  starting transfers between devices  283 us (13%)
  local copies, waits for them, and re-layouts  196 us (9%)
  other arithmetic  172 us (8%)
  loops' own time  30.7 us (1%)
    dot_general x132, matrix products, exact_einsum(): return jnp.einsum(pattern, former, latter, precision=highest)  141 us
    dot_general x20, matrix products, rows_product(): lax.dot_general(former, latter, (((0,), (0,)), ((), ())), preferred_eleme...  135 us
    reduce_scatter x1, waiting for transfers between devices, local(): lax.psum_scatter(all_grads[17], 'dp', scatter_dimension=0, tiled=True)  101 us
    reduce_scatter x1, waiting for transfers between devices, local(): lax.psum_scatter(all_grads[19], 'dp', scatter_dimension=0, tiled=True)  101 us
    all_to_all x11, waiting for transfers between devices, forward_transform(): lax.all_to_all(as_sent(real_twist), 'dp', split_axis=0, concat_axis=1, ti...  99.8 us
    all_to_all x11, waiting for transfers between devices, forward_transform(): lax.all_to_all(signal.reshape(part_count, block_rows, -1).astype(jnp.bflo...  88.5 us
    all_to_all x11, waiting for transfers between devices, forward_transform(): lax.all_to_all(as_sent(imag_twist), 'dp', split_axis=0, concat_axis=1, ti...  85 us
    all_to_all x11, waiting for transfers between devices, inverse_transform(): lax.all_to_all(as_sent(real_twist), 'dp', split_axis=1, concat_axis=0, ti...  83 us
  transfers between devices with their start and end apart: 95, of which 84 were waited for; matrix products, arithmetic and copies ran while one was open for 16% of the time, Pallas kernels for 0%

commit v1 on v0

--- a/solution.py
+++ b/solution.py
@@ -1,8 +1,20 @@
+import functools
+import types
+
 import jax
 import jax.numpy as jnp
+import numpy as np
 from jax import lax
+from jax.experimental import pallas as pl
+from jax.experimental.pallas import tpu as pltpu
 from jax.sharding import PartitionSpec as P
 
+MESH = pl.DeviceIdType.MESH
+LANES = 128
+HALO = 16
+FEATURE_ROWS = 48
+SMALL = 96
+FAR = 6
 EMB = 33
 
 
@@ -365,7 +377,7 @@
     return (grad_state, grads, kernel_grad)
 
 
-def local(
+def local_general(
     inputs,
     cotangent,
     seq_lengths,
@@ -537,6 +549,1704 @@
     )
 
 
+def dot_nn(a, b):
+    return lax.dot_general(a, b, (((1,), (0,)), ((), ())), preferred_element_type=jnp.float32)
+
+
+def dot_nt(a, b):
+    return lax.dot_general(a, b, (((1,), (1,)), ((), ())), preferred_element_type=jnp.float32)
+
+
+def col_sum(a):
+    return jnp.sum(a, axis=0, keepdims=True)
+
+
+def normalized(signal):
+    middle = jnp.mean(signal, axis=-1, keepdims=True)
+    centred = signal - middle
+    spread = jnp.mean(centred * centred, axis=-1, keepdims=True)
+    inverse = lax.rsqrt(spread + norm_epsilon)
+    return (centred * inverse, middle, inverse)
+
+
+def norm_backward(grad, unit, inverse, factor):
+    scaled = grad * factor
+    first = jnp.mean(scaled, axis=-1, keepdims=True)
+    second = jnp.mean(scaled * unit, axis=-1, keepdims=True)
+    return inverse * (scaled - first - unit * second)
+
+
+GELU_ROOT = float(np.sqrt(2.0 / np.pi))
+GELU_CUBE = 0.044715
+
+
+def gelu_half(v, square):
+    return 0.5 + 0.5 * jnp.tanh(v * (GELU_ROOT + (GELU_ROOT * GELU_CUBE) * square))
+
+
+def gelu(v):
+    return v * gelu_half(v, v * v)
+
+
+def gelu_slope(v):
+    square = v * v
+    half = gelu_half(v, square)
+    inner = v * (2.0 * GELU_ROOT + (6.0 * GELU_ROOT * GELU_CUBE) * square)
+    return half * (1.0 + (1.0 - half) * inner)
+
+
+def turned(block):
+    return block.astype(jnp.float32).T.astype(jnp.bfloat16)
+
+
+def aligned(value, by):
+    return pl.multiple_of(value, by)
+
+
+def halves(value):
+    high = value.astype(jnp.bfloat16)
+    return high, (value - high.astype(jnp.float32)).astype(jnp.bfloat16)
+
+
+def fine_left(value):
+    high, low = halves(value)
+    return jnp.concatenate([high, low, high], axis=1)
+
+
+def fine_right(value):
+    high, low = halves(value)
+    return jnp.concatenate([high, high, low], axis=0)
+
+
+def filter_layers(r, part):
+    first = r.filter_one[:, 0, :]
+    rest = jnp.zeros((FEATURE_ROWS - first.shape[0], first.shape[1]), jnp.float32)
+    first = jnp.concatenate([first, rest], axis=0)
+    one = sine_scale * (dot_nn(r.features[part], fine_right(first)) + r.filter_one_bias[...])
+    layer_one = jnp.sin(one)
+    two = dot_nn(fine_left(layer_one), fine_right(r.filter_two[...]))
+    two = sine_scale * (two + r.filter_two_bias[...])
+    return (layer_one, jnp.sin(two), one, two)
+
+
+def chain_kernel(geometry, names, *all_refs):
+    sections, parts, group, rows, width, hidden_width = geometry
+    r = types.SimpleNamespace(**dict(zip(names, all_refs)))
+    total = group * rows
+    blocks = width // LANES
+    share = width // sections
+    held = total // parts
+    s = lax.axis_index("section")
+    e = lax.axis_index("dp")
+    q = e // group
+    flipped = lax.rem(q, 2) == 1
+    i = jnp.where(flipped, group - 1 - e % group, e % group)
+    following = jnp.where(flipped, e - 1, e + 1)
+    preceding = jnp.where(flipped, e + 1, e - 1)
+    mate_core = e + 1 - 2 * lax.rem(e, 2)
+    first_of_group = q * group
+
+    def remote(src, dst, send, recv, section, dp):
+        return pltpu.make_async_remote_copy(
+            src_ref=src,
+            dst_ref=dst,
+            send_sem=send,
+            recv_sem=recv,
+            device_id={"section": section, "dp": dp},
+            device_id_type=MESH,
+        )
+
+    def arrived(dst, recv):
+        remote(dst, dst, recv, recv, s, e).wait_recv()
+
+    def sent(src, send):
+        remote(src, src, send, send, s, e).wait_send()
+
+    def start_to(src, dst, send, recv, section, dp):
+        here = (section == s) & (dp == e)
+
+        @pl.when(here)
+        def _():
+            pltpu.make_async_copy(src, dst, recv).start()
+
+        @pl.when(jnp.logical_not(here))
+        def _():
+            remote(src, dst, send, recv, section, dp).start()
+
+    def sent_to(src, send, section, dp):
+        here = (section == s) & (dp == e)
+
+        @pl.when(jnp.logical_not(here))
+        def _():
+            sent(src, send)
+
+    barrier = pltpu.get_barrier_semaphore()
+    me = s * parts + e
+    devices = sections * parts
+
+    def greet(step, carry):
+        there = lax.rem(me + step, devices)
+        pl.semaphore_signal(
+            barrier,
+            inc=1,
+            device_id={"section": there // parts, "dp": lax.rem(there, parts)},
+            device_id_type=MESH,
+        )
+        return carry
+
+    lax.fori_loop(1, devices, greet, 0)
+
+    def load(there, here, index):
+        copy = pltpu.make_async_copy(there, here, r.load_sem.at[index])
+        copy.start()
+        return copy
+
+    load_in = load(r.w_in, r.v_in, 0)
+    load_out = load(r.w_out, r.v_out, 1)
+    load_up = load(r.w_up, r.v_up, 2)
+    load_down = load(r.w_down, r.v_down, 3)
+
+    pl.semaphore_wait(barrier, devices - 1)
+
+    pos, low_half = e // 2, e % 2
+    micro = r.inputs.shape[0]
+    last = sections - 1
+    halo_there = (low_half == 1) & (pos < group - 1)
+    def holder(m, place):
+        return m * group + (group - 1 - place if m % 2 else place)
+
+    for m in range(micro):
+        dp = holder(m, pos)
+        start_to(
+            r.inputs.at[m],
+            r.in_recv.at[low_half, pl.ds(aligned(s * share, share), share)],
+            r.in_send_sem.at[m],
+            r.in_sem.at[s, low_half],
+            0,
+            dp,
+        )
+
+        @pl.when(halo_there)
+        def _():
+            start_to(
+                r.inputs.at[m],
+                r.in_halo.at[pl.ds(aligned(s * share, share), share)],
+                r.halo_send_sem.at[m],
+                r.halo_sem.at[s],
+                0,
+                holder(m, pos + 1),
+            )
+
+
+    def send_cotangent():
+        for m in range(micro):
+            start_to(
+                r.cot.at[m],
+                r.cot_recv.at[low_half, pl.ds(aligned(s * share, share), share)],
+                r.cot_send_sem.at[m],
+                r.cot_sem.at[s, low_half],
+                last,
+                holder(m, pos),
+            )
+
+    wide = 2 * LANES
+    pieces = width // wide
+    sign = 1.0 - 2.0 * lax.rem(
+        lax.broadcasted_iota(jnp.int32, (rows, 1), 0), jnp.int32(2)
+    ).astype(jnp.float32)
+
+    def chunk_of(k, offset=0):
+        return pl.ds(offset + k * wide, wide)
+
+    def scaled_place(m):
+        place = lax.broadcasted_iota(jnp.int32, (rows, 1), 0) + m * rows
+        return place.astype(jnp.float32) * (1.0 / total)
+
+    def filter_step(m, carry):
+        part = pl.ds(aligned(m * rows, rows), rows)
+        fine = fine_left(filter_layers(r, part)[1])
+        for k in range(pieces):
+            cols = chunk_of(k)
+            raw = dot_nn(fine, fine_right(r.filter_out[:, cols])) + r.filter_out_bias[:, cols]
+            value = raw * jnp.exp(-r.decay[:, cols] * scaled_place(m))
+            spec = dot_nn(r.waves[...], value.astype(jnp.bfloat16))
+            upper, lower = pl.ds(2 * k * wide, wide), pl.ds((2 * k + 1) * wide, wide)
+            even = jnp.where(m > 0, r.gs[pl.ds(0, rows), upper], 0.0)
+            odd = jnp.where(m > 0, r.gs[pl.ds(0, rows), lower], 0.0)
+            r.kspec[m, k, :rows] = (spec[:rows] + sign * odd).astype(jnp.bfloat16)
+            r.kspec[m, k, rows:] = (spec[rows:] - sign * even).astype(jnp.bfloat16)
+            r.gs[pl.ds(0, rows), upper] = spec[:rows]
+            r.gs[pl.ds(0, rows), lower] = spec[rows:]
+        return carry
+
+    @pl.when(s > 0)
+    def _():
+        lax.fori_loop(0, group, filter_step, 0)
+        send_cotangent()
+
+    def order(back):
+        return (group - 1 - i) if back else i
+
+    def mate(n, back):
+        place = (group - 1 - n) if back else n
+        return first_of_group + jnp.where(flipped, group - 1 - place, place)
+
+    def hop(src, back, slot, k, send, there):
+        lanes = r.far_back if back else r.far
+        arrive = r.far_back_sem if back else r.far_sem
+        return remote(src, lanes.at[slot, k], send, arrive.at[slot, k], s, mate(there, back))
+
+    direct = ((0, 2), (0, 1), (1, 3), (2, 3))
+    handed = ((2, 3, 0), (3, 2, 1))
+
+    def send_piece(src, k, back):
+        send = r.near_back_send_sem if back else r.near_send_sem
+        for index, (here, there) in enumerate(direct):
+
+            @pl.when(order(back) == here)
+            def _():
+                hop(src.at[k], back, here, k, send.at[index % 2, k], there).start()
+
+    def pieces_sent(src, back):
+        send = r.near_back_send_sem if back else r.near_send_sem
+        for index, (here, there) in enumerate(direct):
+
+            @pl.when(order(back) == here)
+            def _():
+                for k in range(pieces):
+                    sent(src.at[k], send.at[index % 2, k])
+
+        hand = r.hand_back_send_sem if back else r.hand_send_sem
+        lanes = r.far_back if back else r.far
+        for here, there, slot in handed:
+
+            @pl.when(order(back) == here)
+            def _():
+                for k in range(pieces):
+                    sent(lanes.at[slot, k], hand.at[k])
+
+    def transform(src, into):
+        value = dot_nn(r.waves[...], jnp.concatenate([src[k] for k in range(pieces)], axis=1))
+        for k in range(pieces):
+            into[k] = value[:, k * wide : (k + 1) * wide].astype(jnp.bfloat16)
+
+    def far_from(slot, back):
+        lanes = r.far_back if back else r.far
+        arrive = r.far_back_sem if back else r.far_sem
+        for k in range(pieces):
+            arrived(lanes.at[slot, k], arrive.at[slot, k])
+
+    def transform_far(slot, back):
+        lanes = r.far_back if back else r.far
+        specs = r.wspec if back else r.zspec
+        transform(lanes.at[slot], specs.at[slot])
+
+    def other_chip(back):
+        lanes = r.far_back if back else r.far
+        hand = r.hand_back_send_sem if back else r.hand_send_sem
+        for here, there, slot in handed:
+
+            @pl.when(order(back) == here)
+            def _():
+                arrive = r.far_back_sem if back else r.far_sem
+                for k in range(pieces):
+                    arrived(lanes.at[slot, k], arrive.at[slot, k])
+                    hop(lanes.at[slot, k], back, slot, k, hand.at[k], there).start()
+                transform_far(slot, back)
+                far_from(1 - slot, back)
+                transform_far(1 - slot, back)
+
+    def other_core(back):
+        for n in (1, 3):
+
+            @pl.when(order(back) == n)
+            def _():
+                far_from(n - 1, back)
+                transform_far(n - 1, back)
+
+    fine_rows = 32
+
+    def combine(back, n, sources, first, final):
+        specs = r.wspec if back else r.zspec
+
+        def rows_step(step, carry):
+            k = step // (rows // fine_rows)
+            start = aligned(lax.rem(step, rows // fine_rows) * fine_rows, fine_rows)
+            upper, lower = pl.ds(start, fine_rows), pl.ds(rows + start, fine_rows)
+            lanes = aligned(width + 2 * k * wide, wide)
+            even_place = (pl.ds(start, fine_rows), pl.ds(lanes, wide))
+            odd_place = (pl.ds(start, fine_rows), pl.ds(lanes + wide, wide))
+            even = odd = 0.0
+            if not first:
+                even, odd = r.gs[even_place], r.gs[odd_place]
+            for j in sources:
+                a = specs[j, k, upper].astype(jnp.float32)
+                b = specs[j, k, lower].astype(jnp.float32)
+                u = r.kspec[n - j, k, upper].astype(jnp.float32)
+                v = r.kspec[n - j, k, lower].astype(jnp.float32)
+                if back:
+                    even, odd = even + a * u + b * v, odd + b * u - a * v
+                else:
+                    even, odd = even + a * u - b * v, odd + a * v + b * u
+            if final:
+                r.yspec[k, upper] = even.astype(jnp.bfloat16)
+                r.yspec[k, lower] = odd.astype(jnp.bfloat16)
+            else:
+                r.gs[even_place] = even
+                r.gs[odd_place] = odd
+            return carry
+
+        lax.fori_loop(0, pieces * (rows // fine_rows), rows_step, 0)
+
+    def combine_far(back):
+        for n in (2, 3):
+
+            @pl.when(order(back) == n)
+            def _():
+                combine(back, n, (0, 1), True, False)
+
+    def combine_near(back):
+        for n in range(group):
+
+            @pl.when(order(back) == n)
+            def _():
+                if n < 2:
+                    combine(back, n, range(n + 1), True, True)
+                else:
+                    combine(back, n, range(2, n + 1), False, True)
+
+    def inverse():
+        spec = jnp.concatenate([r.yspec[k] for k in range(pieces)], axis=1)
+        return dot_nn(r.waves_back[...], spec) * (1.0 / rows)
+
+    @pl.when(s > 0)
+    def _():
+        other_chip(False)
+        combine_far(False)
+
+    @pl.when(s == last)
+    def _():
+        length = r.lengths[q]
+        for section in range(sections):
+            for h in range(2):
+                arrived(
+                    r.cot_recv.at[h, pl.ds(section * share, share)], r.cot_sem.at[section, h]
+                )
+        for h in range(2):
+            part = pl.ds(h * (rows // 2), rows // 2)
+            place = lax.broadcasted_iota(jnp.int32, (rows // 2, 1), 0) + i * rows + h * (rows // 2)
+            live = (place < length).astype(jnp.float32)
+            r.g[part] = (turned(r.cot_recv[h]).astype(jnp.float32) * live).astype(jnp.bfloat16)
+
+    @pl.when(s == 0)
+    def _():
+        for section in range(sections):
+            for h in range(2):
+                arrived(
+                    r.in_recv.at[h, pl.ds(section * share, share)], r.in_sem.at[section, h]
+                )
+        for h in range(2):
+            start = HALO + h * held
+            r.x[start : start + held] = turned(r.in_recv[h])
+
+        @pl.when(i > 0)
+        def _():
+            for section in range(sections):
+                arrived(
+                    r.in_halo.at[pl.ds(section * share, share)], r.halo_sem.at[section]
+                )
+            r.x[:HALO] = turned(r.in_halo[...])[held - HALO :]
+
+    @pl.when(s > 0)
+    def _():
+        arrived(r.x.at[pl.ds(HALO, rows)], r.pass_sem.at[0])
+
+        @pl.when(i > 0)
+        def _():
+            arrived(r.x.at[pl.ds(0, HALO)], r.pass_sem.at[1])
+
+    def norm_rows(start, count):
+        unit, middle, inverse = normalized(r.x[pl.ds(start, count)].astype(jnp.float32))
+        r.stats[pl.ds(start, count), 0:1] = middle
+        r.stats[pl.ds(start, count), 1:2] = inverse
+        r.normed[pl.ds(start, count)] = (
+            unit * r.norm_gain[...] + r.norm_bias[...]
+        ).astype(jnp.bfloat16)
+
+    norm_rows(0, HALO)
+    chunk = 128
+
+    def norm_step(step, carry):
+        norm_rows(aligned(HALO + step * chunk, HALO), chunk)
+        return carry
+
+    lax.fori_loop(0, rows // chunk, norm_step, 0)
+    load_in.wait()
+
+    def mix(cols):
+        value = dot_nn(r.normed[...], r.v_in[:, cols]) + r.in_bias[:, cols]
+        r.mixed[pl.ds(HALO, rows), cols] = value[HALO:]
+        r.mixed[:HALO, cols] = jnp.where(i > 0, value[:HALO], 0.0)
+
+    for k in (1, 2):
+        mix(pl.ds(k * width, width))
+
+    def lanes_of(block, offset=0):
+        return pl.ds(aligned(offset + block * LANES, LANES), LANES)
+
+    def short_conv(cols):
+        here = r.mixed[pl.ds(HALO, rows), cols]
+        one = r.mixed[pl.ds(HALO - 1, rows), cols]
+        two = r.mixed[pl.ds(HALO - 2, rows), cols]
+        w = r.short_weight
+        value = w[0, :, cols] * here + w[1, :, cols] * one + w[2, :, cols] * two
+        value = value + r.short_bias[:, cols]
+        r.short[:, cols] = value
+        return value
+
+    for k in range(pieces):
+        gate = short_conv(chunk_of(k, width))
+        value = short_conv(chunk_of(k, 2 * width))
+        r.mid_send[k] = (gate * value).astype(jnp.bfloat16)
+        mix(chunk_of(k))
+        send_piece(r.mid_send, k, False)
+    transform(r.mid_send, r.zspec.at[i])
+    for k in range(pieces):
+        short_conv(chunk_of(k))
+
+    @pl.when(s == 0)
+    def _():
+        lax.fori_loop(0, group, filter_step, 0)
+        send_cotangent()
+
+    @pl.when(s == 0)
+    def _():
+        other_chip(False)
+        combine_far(False)
+
+    other_core(False)
+    combine_near(False)
+    found = inverse()
+    for k in range(pieces):
+        cols = chunk_of(k)
+        middle = r.short[:, chunk_of(k, width)] * r.short[:, chunk_of(k, 2 * width)]
+        conv = found[:, k * wide : (k + 1) * wide] + r.skip_gain[:, cols] * middle
+        r.conv_out[:, cols] = conv
+        r.gated[:, cols] = (r.short[:, cols] * conv).astype(jnp.bfloat16)
+    load_out.wait()
+    r.residual[...] = (
+        dot_nn(r.gated[...], r.v_out[...])
+        + r.out_bias[...]
+        + r.x[pl.ds(HALO, rows)].astype(jnp.float32)
+    )
+
+    def norm_two_step(step, carry):
+        part = pl.ds(aligned(step * chunk, chunk), chunk)
+        value = r.residual[part]
+        unit, middle, inverse = normalized(value)
+        r.stats[part, 2:3] = middle
+        r.stats[part, 3:4] = inverse
+        r.normed_two[part] = (
+            unit * r.second_norm_gain[...] + r.second_norm_bias[...]
+        ).astype(jnp.bfloat16)
+        return carry
+
+    lax.fori_loop(0, rows // chunk, norm_two_step, 0)
+    load_up.wait()
+    load_down.wait()
+
+    feed_steps = hidden_width // width
+    for k in range(feed_steps):
+        cols = pl.ds(k * width, width)
+        value = dot_nn(r.normed_two[...], r.v_up[:, cols]) + r.up_bias[:, cols]
+        r.active[:, cols] = gelu(value).astype(jnp.bfloat16)
+        r.slope[:, cols] = value.astype(jnp.bfloat16)
+    fed = dot_nn(r.active[...], r.v_down[...])
+    r.out[...] = (fed + (r.residual[...] + r.down_bias[...])).astype(jnp.bfloat16)
+
+    def pass_rows(src, dst, send, recv, section, first, turn):
+        @pl.when(jnp.logical_not(first))
+        def _():
+            pl.semaphore_wait(turn, 1)
+
+        remote(src, dst, send, recv, section, e).start()
+
+        @pl.when(first)
+        def _():
+            sent(src, send)
+            pl.semaphore_signal(
+                turn, inc=1, device_id={"section": s, "dp": mate_core}, device_id_type=MESH
+            )
+
+    ahead = lax.rem(i, 2) == 0
+
+    @pl.when(s < last)
+    def _():
+        @pl.when(i < group - 1)
+        def _():
+            remote(
+                r.out.at[pl.ds(rows - HALO, HALO)],
+                r.x.at[pl.ds(0, HALO)],
+                r.pass_send_sem.at[1],
+                r.pass_sem.at[1],
+                s + 1,
+                following,
+            ).start()
+
+        pass_rows(
+            r.out,
+            r.x.at[pl.ds(HALO, rows)],
+            r.pass_send_sem.at[0],
+            r.pass_sem.at[0],
+            s + 1,
+            ahead,
+            r.turn.at[0],
+        )
+
+    def spread(stage, dst, send, recv):
+        for section in range(sections):
+            for h in range(2):
+                start_to(
+                    stage.at[h, pl.ds(section * share, share)],
+                    dst.at[q],
+                    send.at[section, h],
+                    recv.at[q],
+                    section,
+                    2 * i + h,
+                )
+
+    def spread_sent(stage, send):
+        for section in range(sections):
+            for h in range(2):
+                sent_to(
+                    stage.at[h, pl.ds(section * share, share)],
+                    send.at[section, h],
+                    section,
+                    2 * i + h,
+                )
+
+    def slope_step(step, carry):
+        part = pl.ds(aligned(step * HALO, HALO), HALO)
+        r.slope[part] = gelu_slope(r.slope[part].astype(jnp.float32)).astype(jnp.bfloat16)
+        return carry
+
+    lax.fori_loop(0, rows // HALO, slope_step, 0)
+
+    z = e // 2
+    line = parts // 2
+    inner = (z > 0) & (z < line - 1)
+    inwards = jnp.where(z == 0, e + 2, e - 2)
+
+    def give(src, dst, index):
+        return remote(
+            src, dst, r.give_send_sem.at[index], r.give_sem.at[index], s, inwards
+        )
+
+    @pl.when((z == 0) | (z == line - 1))
+    def _():
+        give(r.normed_two, r.far_normed, 0).start()
+
+    side = z // 2
+    across = jnp.where(z < line // 2, e + 2, e - 2)
+    unit = width // parts
+    times = hidden_width // width
+    tall = times * unit
+    side_up, side_down = line * unit, line * tall
+
+    def of_side(ref, which, count):
+        return ref.at[:, pl.ds(aligned(which * count, LANES), count)]
+
+    def cross(src, dst, kind, b):
+        return remote(src, dst, r.cross_send_sem.at[kind, b], r.cross_sem.at[kind, b], s, across)
+
+    def fetch(there, here, index):
+        copy = pltpu.make_async_copy(there, here, r.far_load_sem.at[index])
+        copy.start()
+        return copy
+
+    def each(count, body):
+        def step(k, carry):
+            body(k)
+            return carry
+
+        lax.fori_loop(0, count, step, 0)
+
+    @pl.when(inner)
+    def _():
+        cross(r.normed_two, r.x_normed.at[0], 0, 0).start()
+        arrived(r.far_normed, r.give_sem.at[0])
+        cross(r.far_normed, r.x_normed.at[1], 0, 1).start()
+
+    def work_out_others():
+        copies = [fetch(r.far_normed, r.normed_side.at[0], 0)]
+        for b in range(2):
+            arrived(r.x_normed.at[b], r.cross_sem.at[0, b])
+            copies.append(fetch(r.x_normed.at[b], r.normed_side.at[1 + b], 1 + b))
+        for copy in copies:
+            copy.wait()
+
+        def other_step(step):
+            b, k = step // times, lax.rem(step, times)
+            cols = pl.ds(aligned(k * width, width), width)
+            value = dot_nn(r.normed_side[b], r.v_up[:, cols]) + r.up_bias[:, cols]
+            r.g_side[0] = gelu(value).astype(jnp.bfloat16)
+            low = value.astype(jnp.bfloat16).astype(jnp.float32)
+            r.g_side[1] = gelu_slope(low).astype(jnp.bfloat16)
+            first = fetch(r.g_side.at[0], r.s_active.at[b, :, cols], 0)
+            second = fetch(r.g_side.at[1], r.s_slope.at[b, :, cols], 1)
+            first.wait()
+            second.wait()
+
+        each(3 * times, other_step)
+
+    idle = s < last - 1
+
+    @pl.when(inner & idle)
+    def _():
+        work_out_others()
+
+    @pl.when(s < last)
+    def _():
+        other_chip(True)
+        combine_far(True)
+        arrived(r.g, r.grad_sem)
+
+
+    @pl.when((z == 0) | (z == line - 1))
+    def _():
+        give(r.g, r.far_g, 1).start()
+
+    @pl.when(inner)
+    def _():
+        cross(r.g, r.x_g.at[0], 1, 0).start()
+
+    for k in range(feed_steps):
+        cols = pl.ds(k * width, width)
+        grad_active = dot_nt(r.g[...], r.v_down[cols, :])
+        r.gh[:, cols] = (grad_active * r.slope[:, cols].astype(jnp.float32)).astype(jnp.bfloat16)
+    r.acc[...] = dot_nt(r.gh[...], r.v_up[...])
+
+    def norm_two_back(step, carry):
+        gain_sum, bias_sum, out_sum = carry
+        part = pl.ds(aligned(step * chunk, chunk), chunk)
+        inverse = r.stats[part, 3:4]
+        unit = (r.residual[part] - r.stats[part, 2:3]) * inverse
+        grad = r.acc[part]
+        value = r.g[part].astype(jnp.float32) + norm_backward(
+            grad, unit, inverse, r.second_norm_gain[...]
+        )
+        r.g_res[part] = value
+        low = value.astype(jnp.bfloat16)
+        r.gb[part] = low
+        return (
+            gain_sum + col_sum(grad * unit),
+            bias_sum + col_sum(grad),
+            out_sum + col_sum(low.astype(jnp.float32)),
+        )
+
+    zero = jnp.zeros((1, width), jnp.float32)
+    gain_sum, bias_sum, out_sum = lax.fori_loop(
+        0, rows // chunk, norm_two_back, (zero, zero, zero)
+    )
+    r.v768[3:4] = out_sum
+    r.v768[4:5] = gain_sum
+    r.v768[5:6] = bias_sum
+    r.acc[...] = dot_nt(r.gb[...], r.v_out[...])
+
+    for k in range(pieces):
+        cols = chunk_of(k)
+        grad_conv = r.acc[:, cols] * r.short[:, cols]
+        r.g_conv[:, cols] = grad_conv
+        r.grad_send[k] = grad_conv.astype(jnp.bfloat16)
+        send_piece(r.grad_send, k, True)
+    transform(r.grad_send, r.wspec.at[order(True)])
+    for k in range(pieces):
+        cols = chunk_of(k)
+        r.gs[pl.ds(0, rows), cols] = r.acc[:, cols] * r.conv_out[:, cols]
+    @pl.when(s == last)
+    def _():
+        other_chip(True)
+        combine_far(True)
+
+    other_core(True)
+    combine_near(True)
+    found = inverse()
+    for k in range(pieces):
+        cols = chunk_of(k)
+        gate_cols, value_cols = chunk_of(k, width), chunk_of(k, 2 * width)
+        grad_middle = r.skip_gain[:, cols] * r.g_conv[:, cols] + found[:, k * wide : (k + 1) * wide]
+        r.gs[pl.ds(0, rows), gate_cols] = grad_middle * r.short[:, value_cols]
+        r.gs[pl.ds(0, rows), value_cols] = grad_middle * r.short[:, gate_cols]
+
+    @pl.when(i > 0)
+    def _():
+        remote(
+            r.gs.at[pl.ds(0, 8)],
+            r.gs.at[pl.ds(rows, 8)],
+            r.edge_send_sem,
+            r.edge_sem,
+            s,
+            preceding,
+        ).start()
+
+    @pl.when(i == group - 1)
+    def _():
+        r.gs[pl.ds(rows, 8)] = jnp.zeros((8, 3 * width), jnp.float32)
+
+    @pl.when(i < group - 1)
+    def _():
+        arrived(r.gs.at[pl.ds(rows, 8)], r.edge_sem)
+
+    def mixed_back(cols):
+        here = r.gs[pl.ds(0, rows), cols]
+        w = r.short_weight
+        value = w[0, :, cols] * here
+        value = value + w[1, :, cols] * r.gs[pl.ds(1, rows), cols]
+        value = value + w[2, :, cols] * r.gs[pl.ds(2, rows), cols]
+        r.gm[:, cols] = value.astype(jnp.bfloat16)
+
+    def in_back(k):
+        cols = pl.ds(k * width, width)
+        return dot_nt(r.gm[:, cols], r.v_in[:, cols])
+
+    back = None
+    for third in range(3):
+        for k in range(pieces):
+            mixed_back(chunk_of(k, third * width))
+        if third > 0:
+            back = in_back(third - 1) if back is None else back + in_back(third - 1)
+    r.acc[...] = back + in_back(2)
+
+    def norm_back(step, carry):
+        gain_sum, bias_sum, down_sum = carry
+        part = pl.ds(aligned(step * chunk, chunk), chunk)
+        there = pl.ds(aligned(HALO + step * chunk, HALO), chunk)
+        inverse = r.stats[there, 1:2]
+        unit = (r.x[there].astype(jnp.float32) - r.stats[there, 0:1]) * inverse
+        grad = r.acc[part]
+        value = r.g_res[part] + norm_backward(grad, unit, inverse, r.norm_gain[...])
+        r.g_res[part] = value
+        r.g_pass[part] = value.astype(jnp.bfloat16)
+        return (
+            gain_sum + col_sum(grad * unit),
+            bias_sum + col_sum(grad),
+            down_sum + col_sum(r.g[part].astype(jnp.float32)),
+        )
+
+    gain_sum, bias_sum, down_sum = lax.fori_loop(0, rows // chunk, norm_back, (zero, zero, zero))
+    r.v768[0:1] = gain_sum
+    r.v768[1:2] = bias_sum
+    r.v768[6:7] = down_sum
+    r.v768[7:8] = zero
+
+    @pl.when(s > 0)
+    def _():
+        pass_rows(
+            r.g_pass,
+            r.g,
+            r.grad_send_sem,
+            r.grad_sem,
+            s - 1,
+            jnp.logical_not(ahead),
+            r.turn.at[1],
+        )
+
+
+    @pl.when(s == last)
+    def _():
+        length = r.lengths[q]
+        for h in range(2):
+            part = pl.ds(h * (rows // 2), rows // 2)
+            place = lax.broadcasted_iota(jnp.int32, (rows // 2, 1), 0) + i * rows + h * (rows // 2)
+            live = (place < length).astype(jnp.float32)
+            r.stage[h] = turned(r.out[part].astype(jnp.float32) * live)
+        spread(r.stage, r.outputs, r.show_send_sem, r.show_sem)
+
+    @pl.when(s == 0)
+    def _():
+        for h in range(2):
+            r.stage[h] = r.g_res[pl.ds(h * held, held)].T.astype(jnp.bfloat16)
+        for section in range(sections):
+            for h in range(2):
+                src = r.stage.at[h, pl.ds(section * share, share)]
+                if section == 0:
+                    start_to(
+                        src,
+                        r.input_grad.at[q],
+                        r.grad_show_send_sem.at[0, h],
+                        r.grad_show_sem.at[q],
+                        0,
+                        2 * i + h,
+                    )
+                else:
+                    remote(
+                        src,
+                        r.grad_relay.at[h],
+                        r.grad_show_send_sem.at[section, h],
+                        r.grad_relay_sem.at[h],
+                        section,
+                        e,
+                    ).start()
+
+    c = lax.rem(e, 2)
+    half_rows = line * unit
+    first_down, out_job, first_in, small_job = times, 2 * times, 2 * times + 1, 2 * times + 4
+
+    def up_rows(k, start, count):
+        cols = pl.ds(aligned(k * width, width), width)
+        return r.v_up.at[pl.ds(aligned(start, HALO), count), cols]
+
+    def down_rows(k, start, count):
+        return r.v_down.at[pl.ds(aligned(k * width + start, HALO), count)]
+
+    def out_rows(k, start, count):
+        return r.v_out.at[pl.ds(aligned(start, HALO), count)]
+
+    def in_rows(k, start, count):
+        cols = pl.ds(aligned(k * width, width), width)
+        return r.v_in.at[pl.ds(aligned(start, HALO), count), cols]
+
+    def own_part(rows_of, k, owner):
+        return rows_of(k, c * half_rows + owner * unit, unit)
+
+    def to_mate(rows_of, k, j):
+        src = rows_of(k, (1 - c) * half_rows, half_rows)
+        remote(src, r.pair.at[j], r.pair_send_sem.at[j], r.pair_sem.at[j], s, mate_core).start()
+
+    def add_to(ref, value):
+        ref[...] = (ref[...].astype(jnp.float32) + value.astype(jnp.float32)).astype(ref.dtype)
+
+    def merge_mate(rows_of, k, j):
+        arrived(r.pair.at[j], r.pair_sem.at[j])
+        copy = pltpu.make_async_copy(r.pair.at[j], r.pair_here, r.pair_load_sem)
+        copy.start()
+        copy.wait()
+        for owner in range(line):
+            add_to(own_part(rows_of, k, owner), r.pair_here[pl.ds(owner * unit, unit)])
+
+    def send_line(src, dst, j, owner, slot, to):
+        remote(src, dst, r.line_send_sem.at[j, owner], r.line_sem.at[j, slot], s, to).start()
+
+    def line_slot(at, owner, rightward):
+        return owner if rightward or owner < at else line
+
+    def send_full(rows_of, k, j, lines, n, at, owner, add):
+        rightward = owner > at
+        src = own_part(rows_of, k, owner)
+        if add:
+            slot = line_slot(at, owner, rightward)
+            arrived(lines.at[n, slot], r.line_sem.at[j, slot])
+            add_to(src, lines[n, slot])
+        after = at + (1 if rightward else -1)
+        slot = line_slot(after, owner, rightward)
+        send_line(src, lines.at[n, slot], j, owner, slot, e + 2 * (after - at))
+
+    def start_full(rows_of, k, j, lines, n):
+        for at in (0, line - 1):
+
+            @pl.when(z == at)
+            def _():
+                for owner in sorted(range(line), key=lambda o: -abs(o - at)):
+                    if owner != at:
+                        send_full(rows_of, k, j, lines, n, at, owner, False)
+
+    def pass_full(rows_of, k, j, lines, n, steps):
+        for at in range(1, line - 1):
+
+            @pl.when(z == at)
+            def _():
+                if at == steps:
+                    for owner in range(line - 1, at, -1):
+                        send_full(rows_of, k, j, lines, n, at, owner, True)
+                if line - 1 - at == steps:
+                    for owner in range(at):
+                        send_full(rows_of, k, j, lines, n, at, owner, True)
+
+    def store_partial(rows_of, k, value):
+        for owner in range(parts):
+            piece = value[owner * unit : (owner + 1) * unit]
+            start = (owner % 2) * half_rows + (owner // 2) * unit
+            rows_of(k, start, unit)[...] = piece.astype(jnp.bfloat16)
+
+    kept = pl.ds(HALO, rows)
+
+    store_partial(out_rows, 0, rows_product(r.gated[...], r.gb[...]))
+    to_mate(out_rows, 0, out_job)
+
+    def in_job(k):
+        cols = pl.ds(aligned(k * width, width), width)
+        store_partial(in_rows, k, rows_product(r.normed[kept], r.gm[:, cols]))
+        to_mate(in_rows, k, first_in + k)
+
+    each(3, in_job)
+    merge_mate(out_rows, 0, out_job)
+    start_full(out_rows, 0, out_job, r.full_line, 0)
+
+    def merge_in(k):
+        merge_mate(in_rows, k, first_in + k)
+        start_full(in_rows, k, first_in + k, r.full_line, 1 + k)
+
+    each(3, merge_in)
+
+    def sums_step(b, carry):
+        cols = lanes_of(b)
+        here = r.gs[pl.ds(0, rows), cols]
+        r.v2304[0:1, cols] = col_sum(r.gm[:, cols].astype(jnp.float32))
+        for tap in range(3):
+            r.v2304[1 + tap : 2 + tap, cols] = col_sum(
+                here * r.mixed[pl.ds(HALO - tap, rows), cols]
+            )
+        r.v2304[4:5, cols] = col_sum(here)
+        return carry
+
+    lax.fori_loop(0, 3 * blocks, sums_step, 0)
+    r.v2304[5:8] = jnp.zeros((3, 3 * width), jnp.float32)
+    for k in range(pieces):
+        cols = chunk_of(k)
+        middle = r.short[:, chunk_of(k, width)] * r.short[:, chunk_of(k, 2 * width)]
+        r.v768[2:3, cols] = col_sum(r.g_conv[:, cols] * middle)
+    for step in range(hidden_width // width):
+        cols = pl.ds(step * width, width)
+        r.v3072[:, cols] = col_sum(r.gh[:, cols].astype(jnp.float32))
+    mine = order(True)
+
+    def filter_rows(step, carry):
+        m = step // (pieces * (rows // fine_rows))
+        k = lax.rem(step // (rows // fine_rows), pieces)
+        start = aligned(lax.rem(step, rows // fine_rows) * fine_rows, fine_rows)
+        upper, lower = pl.ds(start, fine_rows), pl.ds(rows + start, fine_rows)
+        a = r.wspec[mine, k, upper].astype(jnp.float32)
+        b = r.wspec[mine, k, lower].astype(jnp.float32)
+        turn = 1.0 - 2.0 * lax.rem(
+            lax.broadcasted_iota(jnp.int32, (fine_rows, 1), 0), jnp.int32(2)
+        ).astype(jnp.float32)
+        turn = jnp.where(m < i, turn, 0.0)
+
+        def against(j):
+            u = r.zspec[j, k, upper].astype(jnp.float32)
+            v = r.zspec[j, k, lower].astype(jnp.float32)
+            return (a * u + b * v, b * u - a * v)
+
+        even, odd = against(i - m)
+        next_even, next_odd = against(jnp.maximum(i - m - 1, 0))
+        r.zspec[i - m, k, upper] = (even - turn * next_odd).astype(jnp.bfloat16)
+        r.zspec[i - m, k, lower] = (odd + turn * next_even).astype(jnp.bfloat16)
+        return carry
+
+    lax.fori_loop(0, (i + 1) * pieces * (rows // fine_rows), filter_rows, 0)
+    quarter = half_rows // 2
+
+    def side_part(rows_of, k, h):
+        return rows_of(k, c * quarter + h * unit, unit)
+
+    def side_to_mate(rows_of, k, j):
+        src = rows_of(k, (1 - c) * quarter, quarter)
+        return remote(
+            src,
+            r.pair.at[j, pl.ds(0, quarter)],
+            r.pair_send_sem.at[j],
+            r.pair_sem.at[j],
+            s,
+            mate_core,
+        )
+
+    def side_edge(rows_of, k, j):
+        edge = jnp.where(side == 0, 0, line - 1)
+        to = jnp.where(side == 0, e - 2, e + 2)
+        return remote(
+            side_part(rows_of, k, side),
+            r.inner_line.at[j],
+            r.line_send_sem.at[j, edge],
+            r.line_sem.at[j, 0],
+            s,
+            to,
+        )
+
+    def side_merge(rows_of, k, j):
+        here = pl.ds(0, quarter)
+        arrived(r.pair.at[j, here], r.pair_sem.at[j])
+        copy = pltpu.make_async_copy(r.pair.at[j, here], r.pair_here.at[here], r.pair_load_sem)
+        copy.start()
+        copy.wait()
+        for h in range(2):
+            add_to(side_part(rows_of, k, h), r.pair_here[pl.ds(h * unit, unit)])
+        side_edge(rows_of, k, j).start()
+
+    def side_store(rows_of, k, share_index, piece):
+        start = lax.rem(share_index, 2) * quarter + (share_index // 2) * unit
+        rows_of(k, start, unit)[...] = piece.astype(jnp.bfloat16)
+
+    @pl.when(inner & jnp.logical_not(idle))
+    def _():
+        work_out_others()
+
+    @pl.when(inner)
+    def _():
+        arrived(r.far_g, r.give_sem.at[1])
+        cross(r.far_g, r.x_g.at[1], 1, 1).start()
+        copies = [fetch(r.far_g, r.x.at[kept], 0)]
+        for b in range(2):
+            arrived(r.x_g.at[b], r.cross_sem.at[1, b])
+            copies.append(fetch(r.x_g.at[b], r.g_side.at[b], 1 + b))
+        for copy in copies:
+            copy.wait()
+
+        def staged(b):
+            return r.slope.at[:, pl.ds(b * width, width)]
+
+        def up_side(k):
+            cols = pl.ds(aligned(k * width, width), width)
+            loads = [fetch(r.s_slope.at[b, :, cols], staged(b), b) for b in range(3)]
+            own = of_side(r.normed_two, side, side_up)
+            value = rows_product(own[...], r.gh[:, cols])
+            for b, grads in enumerate((r.x.at[kept], r.g_side.at[0], r.g_side.at[1])):
+                grad = dot_nt(grads[...], r.v_down[cols, :])
+                loads[b].wait()
+                grad = (grad * staged(b)[...].astype(jnp.float32)).astype(jnp.bfloat16)
+                value = value + rows_product(of_side(r.normed_side.at[b], side, side_up)[...], grad)
+            for n in range(line):
+                side_store(up_rows, k, n, value[n * unit : (n + 1) * unit])
+            side_to_mate(up_rows, k, k).start()
+
+            @pl.when(k > 0)
+            def _():
+                side_merge(up_rows, k - 1, k - 1)
+
+        each(times, up_side)
+        pass_full(out_rows, 0, out_job, r.full_line, 0, 1)
+        homes = (r.slope.at[:, :side_down], r.slope.at[:, side_down:], r.gh.at[:, :side_down])
+        copies = [
+            fetch(of_side(r.s_active.at[b], side, side_down), homes[b], b) for b in range(3)
+        ]
+        side_merge(up_rows, times - 1, times - 1)
+        for copy in copies:
+            copy.wait()
+
+        def down_side(n):
+            cols = pl.ds(aligned(n * tall, tall), tall)
+            second = pl.ds(aligned(side_down + n * tall, tall), tall)
+            mine = pl.ds(aligned(side * side_down + n * tall, tall), tall)
+            value = rows_product(r.active[:, mine], r.g[...])
+            value = value + rows_product(r.slope[:, cols], r.x[kept])
+            value = value + rows_product(r.slope[:, second], r.g_side[0])
+            value = value + rows_product(r.gh[:, cols], r.g_side[1])
+            for k in range(times):
+                side_store(down_rows, k, n, value[unit * k : unit * (k + 1)])
+
+        each(line, down_side)
+        each(times, lambda k: side_to_mate(down_rows, k, first_down + k).start())
+        pass_full(in_rows, 0, first_in, r.full_line, 1, 1)
+        each(times, lambda k: side_merge(down_rows, k, first_down + k))
+
+    filt = r.filter_two.shape[0]
+
+    def filter_back(step, carry):
+        g_one, g_one_bias, g_two, g_two_bias, g_out, g_out_bias = carry
+        part = pl.ds(aligned(step * rows, rows), rows)
+        layer_one, layer_two, one, two = filter_layers(r, part)
+        low_two = layer_two.astype(jnp.bfloat16)
+        back = jnp.zeros((rows, filt), jnp.float32)
+        out_parts, bias_parts = [], []
+        for k in range(pieces):
+            cols = pl.ds(k * wide, wide)
+            grad = dot_nn(r.waves_back[...], r.zspec[i - step, k]) * (1.0 / rows)
+            grad = grad * jnp.exp(-r.decay[:, cols] * scaled_place(step))
+            low = grad.astype(jnp.bfloat16)
+            back = back + dot_nt(low, r.filter_out[:, cols].astype(jnp.bfloat16))
+            out_parts.append(rows_product(low_two, low))
+            bias_parts.append(col_sum(grad))
+        back = back * (sine_scale * jnp.cos(two))
+        low = back.astype(jnp.bfloat16)
+        front = dot_nt(low, r.filter_two[...].astype(jnp.bfloat16)) * (sine_scale * jnp.cos(one))
+        high = r.features[part, :FEATURE_ROWS]
+        return (
+            g_one + rows_product(front.astype(jnp.bfloat16), high),
+            g_one_bias + col_sum(front),
+            g_two + rows_product(layer_one.astype(jnp.bfloat16), low),
+            g_two_bias + col_sum(back),
+            g_out + jnp.concatenate(out_parts, axis=1),
+            g_out_bias + jnp.concatenate(bias_parts, axis=1),
+        )
+
+    shapes = (
+        (filt, FEATURE_ROWS),
+        (1, filt),
+        (filt, filt),
+        (1, filt),
+        (filt, width),
+        (1, width),
+    )
+    zeros = tuple(jnp.zeros(shape, jnp.float32) for shape in shapes)
+    g_one, g_one_bias, g_two, g_two_bias, g_out, g_out_bias = lax.fori_loop(
+        0, i + 1, filter_back, zeros
+    )
+    r.small[...] = jnp.zeros(r.small.shape, jnp.float32)
+    few = filt // parts
+    for owner in range(parts):
+        y, x = owner % 2, owner // 2
+        r.small[y, x, 0:8, :unit] = r.v768[:, unit * owner : unit * (owner + 1)]
+        r.small[y, x, 7:8, :unit] = g_out_bias[:, unit * owner : unit * (owner + 1)]
+        for m in range(3):
+            start = 3 * unit * owner + unit * m
+            r.small[y, x, 8 * (m + 1) : 8 * (m + 2), :unit] = r.v2304[:, start : start + unit]
+            start = 3 * LANES * owner + LANES * m
+            r.small[y, x, 8 * m + 13 : 8 * m + 14] = r.v3072[:, start : start + LANES]
+        mine = slice(few * owner, few * (owner + 1))
+        r.small[y, x, 14:15, :few] = g_one_bias[:, mine]
+        r.small[y, x, 15:16, :few] = g_two_bias[:, mine]
+        r.small[y, x, 32 : 32 + few, : g_one.shape[1]] = g_one[mine]
+        r.small[y, x, 40 : 40 + few, :filt] = g_two[mine]
+        for b in range(blocks):
+            row = 48 + 8 * b
+            r.small[y, x, row : row + few] = g_out[mine, b * LANES : (b + 1) * LANES]
+
+
+    def small_rows(k, start, count):
+        return r.small.at[start // half_rows, lax.rem(start, half_rows) // unit]
+
+    remote(
+        r.small.at[1 - c],
+        r.small_pair,
+        r.pair_send_sem.at[small_job],
+        r.pair_sem.at[small_job],
+        s,
+        mate_core,
+    ).start()
+    arrived(r.small_pair, r.pair_sem.at[small_job])
+    r.small[c] += r.small_pair[...]
+    start_full(small_rows, 0, small_job, r.small_line, 0)
+
+    def arrive_full(j, lines, n, into):
+        for at in range(line):
+            slots = ([at] if at > 0 else []) + ([line] if at < line - 1 else [])
+
+            @pl.when(z == at)
+            def _():
+                for slot in slots:
+                    arrived(lines.at[n, slot], r.line_sem.at[j, slot])
+                    into[...] += lines[n, slot].astype(jnp.float32)
+
+    depth = r.ready.shape[0]
+
+    def to_result(j, there):
+        slot = lax.rem(j, depth)
+        return pltpu.make_async_copy(r.ready.at[slot], there, r.result_sem.at[slot])
+
+    def free_result(j):
+        @pl.when(j >= depth)
+        def _():
+            to_result(j, r.out_grad).wait()
+
+    def finish_inner(rows_of, k, j, there):
+        free_result(j)
+        into = r.ready.at[lax.rem(j, depth)]
+
+        @pl.when(inner)
+        def _():
+            into[...] = side_part(rows_of, k, 1 - side)[...].astype(jnp.float32)
+
+        @pl.when(jnp.logical_not(inner))
+        def _():
+            arrived(r.inner_line.at[j], r.line_sem.at[j, 0])
+            into[...] = r.inner_line[j].astype(jnp.float32)
+
+        to_result(j, there).start()
+
+    def finish_full(rows_of, k, j, n, there):
+        free_result(j)
+        into = r.ready.at[lax.rem(j, depth)]
+        into[...] = own_part(rows_of, k, z)[...].astype(jnp.float32)
+        arrive_full(j, r.full_line, n, into)
+        to_result(j, there).start()
+
+    def wide_place(ref, k):
+        return ref.at[:, pl.ds(aligned(k * width, width), width)]
+
+    def tall_place(ref, k):
+        return ref.at[pl.ds(aligned(k * unit, HALO), unit)]
+
+    each(times, lambda k: finish_inner(up_rows, k, k, wide_place(r.up_grad, k)))
+
+    @pl.when(inner)
+    def _():
+        each(2, lambda k: pass_full(in_rows, 1 + k, first_in + 1 + k, r.full_line, 2 + k, 1))
+        pass_full(small_rows, 0, small_job, r.small_line, 0, 1)
+
+        for steps in range(2, line - 1):
+            pass_full(out_rows, 0, out_job, r.full_line, 0, steps)
+            each(3, lambda k: pass_full(in_rows, k, first_in + k, r.full_line, 1 + k, steps))
+            pass_full(small_rows, 0, small_job, r.small_line, 0, steps)
+
+    each(
+        times, lambda k: finish_inner(down_rows, k, first_down + k, tall_place(r.down_grad, k))
+    )
+    finish_full(out_rows, 0, out_job, 0, r.out_grad)
+    each(3, lambda k: finish_full(in_rows, k, first_in + k, 1 + k, wide_place(r.in_grad, k)))
+    for j in range(small_job - depth, small_job):
+        to_result(j, r.out_grad).wait()
+    r.small_sum[...] = r.small[c, z]
+    arrive_full(small_job, r.small_line, 0, r.small_sum)
+    got = r.small_sum
+    for row, out in enumerate(
+        (
+            r.norm_gain_grad,
+            r.norm_bias_grad,
+            r.skip_gain_grad,
+            r.out_bias_grad,
+            r.second_gain_grad,
+            r.second_bias_grad,
+            r.down_bias_grad,
+            r.filter_out_bias_grad,
+        )
+    ):
+        out[...] = got[row : row + 1, :unit]
+    for m in range(3):
+        lanes = slice(unit * m, unit * (m + 1))
+        r.in_bias_grad[:, lanes] = got[8 * (m + 1) : 8 * (m + 1) + 1, :unit]
+        for tap in range(3):
+            row = 8 * (m + 1) + 1 + tap
+            r.short_weight_grad[tap, :, lanes] = got[row : row + 1, :unit]
+        r.short_bias_grad[:, lanes] = got[8 * (m + 1) + 4 : 8 * (m + 1) + 5, :unit]
+        r.up_bias_grad[:, LANES * m : LANES * (m + 1)] = got[8 * m + 13 : 8 * m + 14]
+    r.filter_one_bias_grad[...] = got[14:15, :few]
+    r.filter_two_bias_grad[...] = got[15:16, :few]
+    r.filter_one_grad[...] = got[32 : 32 + few, : r.filter_one_grad.shape[1]]
+    r.filter_two_grad[...] = got[40 : 40 + few, :filt]
+    for b in range(blocks):
+        r.filter_out_grad[:, b * LANES : (b + 1) * LANES] = got[48 + 8 * b : 48 + 8 * b + few]
+
+    def line_sent(j, owner, src):
+        sent(src, r.line_send_sem.at[j, owner])
+
+    def sends_end(rows_of, k, j):
+        for owner in range(line):
+
+            @pl.when(z != owner)
+            def _():
+                line_sent(j, owner, own_part(rows_of, k, owner))
+
+    def mate_sent(rows_of, k, j):
+        sent(rows_of(k, (1 - c) * half_rows, half_rows), r.pair_send_sem.at[j])
+
+    @pl.when(inner)
+    def _():
+        cross(r.normed_two, r.x_normed.at[0], 0, 0).wait_send()
+        cross(r.far_normed, r.x_normed.at[1], 0, 1).wait_send()
+        cross(r.g, r.x_g.at[0], 1, 0).wait_send()
+        cross(r.far_g, r.x_g.at[1], 1, 1).wait_send()
+        for rows_of, first in ((up_rows, 0), (down_rows, first_down)):
+
+            def end_side(k):
+                side_to_mate(rows_of, k, first + k).wait_send()
+                side_edge(rows_of, k, first + k).wait_send()
+
+            each(times, end_side)
+
+    mate_sent(out_rows, 0, out_job)
+    sends_end(out_rows, 0, out_job)
+
+    def end_in(k):
+        mate_sent(in_rows, k, first_in + k)
+        sends_end(in_rows, k, first_in + k)
+
+    each(3, end_in)
+    sent(r.small.at[1 - c], r.pair_send_sem.at[small_job])
+    sends_end(small_rows, 0, small_job)
+
+    @pl.when(s == 0)
+    def _():
+        for section in range(sections):
+            for h in range(2):
+                src = r.stage.at[h, pl.ds(section * share, share)]
+                if section == 0:
+                    sent_to(src, r.grad_show_send_sem.at[0, h], 0, 2 * i + h)
+                else:
+                    sent(src, r.grad_show_send_sem.at[section, h])
+
+    @pl.when(s > 0)
+    def _():
+        for h in range(2):
+            arrived(r.grad_relay.at[h], r.grad_relay_sem.at[h])
+            start_to(
+                r.grad_relay.at[h],
+                r.input_grad.at[q],
+                r.grad_hand_sem.at[h],
+                r.grad_show_sem.at[q],
+                s,
+                2 * i + h,
+            )
+        for h in range(2):
+            sent_to(r.grad_relay.at[h], r.grad_hand_sem.at[h], s, 2 * i + h)
+
+    for m in range(micro):
+        arrived(r.input_grad.at[m], r.grad_show_sem.at[m])
+
+    for m in range(micro):
+        dp = holder(m, pos)
+        sent_to(r.inputs.at[m], r.in_send_sem.at[m], 0, dp)
+        sent_to(r.cot.at[m], r.cot_send_sem.at[m], last, dp)
+
+        @pl.when(halo_there)
+        def _():
+            sent_to(r.inputs.at[m], r.halo_send_sem.at[m], 0, holder(m, pos + 1))
+
+    @pl.when(jnp.logical_not(inner))
+    def _():
+        give(r.normed_two, r.far_normed, 0).wait_send()
+        give(r.g, r.far_g, 1).wait_send()
+
+    pieces_sent(r.mid_send, False)
+    pieces_sent(r.grad_send, True)
+
+    @pl.when(i > 0)
+    def _():
+        sent(r.gs.at[pl.ds(0, 8)], r.edge_send_sem)
+
+    @pl.when(s < last)
+    def _():
+        @pl.when(jnp.logical_not(ahead))
+        def _():
+            sent(r.out, r.pass_send_sem.at[0])
+
+        @pl.when(i < group - 1)
+        def _():
+            sent(r.out.at[pl.ds(rows - HALO, HALO)], r.pass_send_sem.at[1])
+
+    @pl.when(s == last)
+    def _():
+        spread_sent(r.stage, r.show_send_sem)
+
+    @pl.when((s > 0) & ahead)
+    def _():
+        sent(r.g_pass, r.grad_send_sem)
+
+    for m in range(micro):
+        arrived(r.outputs.at[m], r.show_sem.at[m])
+
+
+def chain_call(geometry, operands):
+    sections, parts, group, rows, width, hidden_width = geometry
+    total = group * rows
+    blocks = width // LANES
+    share = width // sections
+    wide = 2 * LANES
+    pieces = width // wide
+    micro, _, held = operands["inputs"].shape
+    unit = width // parts
+    line = parts // 2
+    times = hidden_width // width
+    filt = operands["filter_two"].shape[0]
+    few = filt // parts
+    f32, bf16 = jnp.float32, jnp.bfloat16
+    anywhere = pl.BlockSpec(memory_space=pl.ANY)
+    vmem = pl.BlockSpec(memory_space=pltpu.VMEM)
+    smem = pl.BlockSpec(memory_space=pltpu.SMEM)
+    in_specs = [anywhere] * FAR + [smem] + [vmem] * (len(operands) - FAR - 1)
+    outs = dict(
+        outputs=((micro, share, held), bf16, anywhere),
+        input_grad=((micro, share, held), bf16, anywhere),
+        norm_gain_grad=((1, unit), f32, vmem),
+        norm_bias_grad=((1, unit), f32, vmem),
+        in_grad=((unit, 3 * width), f32, anywhere),
+        in_bias_grad=((1, 3 * unit), f32, vmem),
+        short_weight_grad=((3, 1, 3 * unit), f32, vmem),
+        short_bias_grad=((1, 3 * unit), f32, vmem),
+        filter_one_grad=((few, EMB), f32, vmem),
+        filter_one_bias_grad=((1, few), f32, vmem),
+        filter_two_grad=((few, filt), f32, vmem),
+        filter_two_bias_grad=((1, few), f32, vmem),
+        filter_out_grad=((few, width), f32, vmem),
+        filter_out_bias_grad=((1, unit), f32, vmem),
+        skip_gain_grad=((1, unit), f32, vmem),
+        out_grad=((unit, width), f32, anywhere),
+        out_bias_grad=((1, unit), f32, vmem),
+        second_gain_grad=((1, unit), f32, vmem),
+        second_bias_grad=((1, unit), f32, vmem),
+        up_grad=((unit, hidden_width), f32, anywhere),
+        up_bias_grad=((1, times * unit), f32, vmem),
+        down_grad=((times * unit, width), f32, anywhere),
+        down_bias_grad=((1, unit), f32, vmem),
+        far_normed=((rows, width), bf16, anywhere),
+        far_g=((rows, width), bf16, anywhere),
+        pair=((2 * times + 4, line * unit, width), bf16, anywhere),
+        x_normed=((2, rows, width), bf16, anywhere),
+        x_g=((2, rows, width), bf16, anywhere),
+        s_active=((3, rows, hidden_width), bf16, anywhere),
+        s_slope=((3, rows, hidden_width), bf16, anywhere),
+        grad_relay=((2, share, held), bf16, anywhere),
+    )
+    dma = pltpu.SemaphoreType.DMA
+    scratch = dict(
+        v_in=pltpu.VMEM((width, 3 * width), bf16),
+        v_out=pltpu.VMEM((width, width), bf16),
+        v_up=pltpu.VMEM((width, hidden_width), bf16),
+        v_down=pltpu.VMEM((hidden_width, width), bf16),
+        x=pltpu.VMEM((HALO + rows, width), bf16),
+        normed=pltpu.VMEM((HALO + rows, width), bf16),
+        mixed=pltpu.VMEM((HALO + rows, 3 * width), f32),
+        short=pltpu.VMEM((rows, 3 * width), f32),
+        mid_send=pltpu.VMEM((pieces, rows, wide), bf16),
+        grad_send=pltpu.VMEM((pieces, rows, wide), bf16),
+        far=pltpu.VMEM((group - 1, pieces, rows, wide), bf16),
+        far_back=pltpu.VMEM((group - 1, pieces, rows, wide), bf16),
+        kspec=pltpu.VMEM((group, pieces, 2 * rows, wide), bf16),
+        zspec=pltpu.VMEM((group, pieces, 2 * rows, wide), bf16),
+        wspec=pltpu.VMEM((group, pieces, 2 * rows, wide), bf16),
+        yspec=pltpu.VMEM((pieces, 2 * rows, wide), bf16),
+        conv_out=pltpu.VMEM((rows, width), f32),
+        gated=pltpu.VMEM((rows, width), bf16),
+        residual=pltpu.VMEM((rows, width), f32),
+        normed_two=pltpu.VMEM((rows, width), bf16),
+        slope=pltpu.VMEM((rows, hidden_width), bf16),
+        active=pltpu.VMEM((rows, hidden_width), bf16),
+        acc=pltpu.VMEM((rows, width), f32),
+        out=pltpu.VMEM((rows, width), bf16),
+        g=pltpu.VMEM((rows, width), bf16),
+        gh=pltpu.VMEM((rows, hidden_width), bf16),
+        g_res=pltpu.VMEM((rows, width), f32),
+        gb=pltpu.VMEM((rows, width), bf16),
+        g_conv=pltpu.VMEM((rows, width), f32),
+        gs=pltpu.VMEM((rows + 8, 3 * width), f32),
+        gm=pltpu.VMEM((rows, 3 * width), bf16),
+        g_pass=pltpu.VMEM((rows, width), bf16),
+        in_recv=pltpu.VMEM((2, width, held), bf16),
+        in_halo=pltpu.VMEM((width, held), bf16),
+        cot_recv=pltpu.VMEM((2, width, held), bf16),
+        stage=pltpu.VMEM((2, width, held), bf16),
+        load_sem=dma((4,)),
+        v768=pltpu.VMEM((8, width), f32),
+        v2304=pltpu.VMEM((8, 3 * width), f32),
+        v3072=pltpu.VMEM((1, hidden_width), f32),
+        normed_side=pltpu.VMEM((3, rows, width), bf16),
+        g_side=pltpu.VMEM((2, rows, width), bf16),
+        pair_here=pltpu.VMEM((line * unit, width), bf16),
+        inner_line=pltpu.VMEM((2 * times, unit, width), bf16),
+        full_line=pltpu.VMEM((4, line + 1, unit, width), bf16),
+        small=pltpu.VMEM((2, line, SMALL, LANES), f32),
+        small_pair=pltpu.VMEM((line, SMALL, LANES), f32),
+        small_line=pltpu.VMEM((1, line + 1, SMALL, LANES), f32),
+        small_sum=pltpu.VMEM((SMALL, LANES), f32),
+        ready=pltpu.VMEM((3, unit, width), f32),
+        stats=pltpu.VMEM((HALO + rows, 4), f32),
+        pair_send_sem=dma((2 * times + 5,)),
+        pair_sem=dma((2 * times + 5,)),
+        pair_load_sem=dma,
+        line_send_sem=dma((2 * times + 5, line)),
+        line_sem=dma((2 * times + 5, line + 1)),
+        far_load_sem=dma((6,)),
+        cross_send_sem=dma((2, 2)),
+        cross_sem=dma((2, 2)),
+        result_sem=dma((3,)),
+        grad_show_send_sem=dma((sections, 2)),
+        grad_show_sem=dma((micro,)),
+        grad_relay_sem=dma((2,)),
+        grad_hand_sem=dma((2,)),
+        in_send_sem=dma((micro,)),
+        in_sem=dma((sections, 2)),
+        halo_send_sem=dma((micro,)),
+        halo_sem=dma((sections,)),
+        cot_send_sem=dma((micro,)),
+        cot_sem=dma((sections, 2)),
+        near_send_sem=dma((2, pieces)),
+        near_back_send_sem=dma((2, pieces)),
+        hand_send_sem=dma((pieces,)),
+        hand_back_send_sem=dma((pieces,)),
+        far_sem=dma((group - 1, pieces)),
+        far_back_sem=dma((group - 1, pieces)),
+        give_send_sem=dma((2,)),
+        give_sem=dma((2,)),
+        pass_send_sem=dma((2,)),
+        pass_sem=dma((2,)),
+        turn=pltpu.SemaphoreType.REGULAR((2,)),
+        grad_send_sem=dma,
+        grad_sem=dma,
+        edge_send_sem=dma,
+        edge_sem=dma,
+        show_send_sem=dma((sections, 2)),
+        show_sem=dma((micro,)),
+    )
+    names = tuple(operands) + tuple(outs) + tuple(scratch)
+    results = pl.pallas_call(
+        functools.partial(chain_kernel, geometry, names),
+        out_shape=[jax.ShapeDtypeStruct(shape, dtype) for shape, dtype, _ in outs.values()],
+        in_specs=in_specs,
+        out_specs=[spec for _, _, spec in outs.values()],
+        scratch_shapes=list(scratch.values()),
+        compiler_params=pltpu.CompilerParams(
+            collective_id=0, has_side_effects=True, vmem_limit_bytes=62 * 1024 * 1024
+        ),
+        name="chain",
+    )(*operands.values())
+    return types.SimpleNamespace(**dict(zip(outs, results)))
+
+
+def store_kernel(count, widened, *refs):
+    source, result, held, sem = refs[:count], refs[count : 2 * count], refs[2 * count : -2], refs[-1]
+    wide = refs[-2]
+    loads = [pltpu.make_async_copy(source[k], held[k], sem.at[0, k]) for k in range(count)]
+    stores = [
+        pltpu.make_async_copy(wide if k == widened else held[k], result[k], sem.at[1, k])
+        for k in range(count)
+    ]
+    for copy in loads:
+        copy.start()
+    for k in range(count):
+        loads[k].wait()
+        if k == widened:
+            wide[...] = held[k][...].astype(jnp.float32)
+        stores[k].start()
+    for copy in stores:
+        copy.wait()
+
+
+def store_call(arrays, widened=1):
+    anywhere = pl.BlockSpec(memory_space=pl.ANY)
+    count = len(arrays)
+    types_out = [jnp.float32 if k == widened else array.dtype for k, array in enumerate(arrays)]
+    return pl.pallas_call(
+        functools.partial(store_kernel, count, widened),
+        out_shape=[
+            jax.ShapeDtypeStruct(array.shape, dtype) for array, dtype in zip(arrays, types_out)
+        ],
+        in_specs=[anywhere] * count,
+        out_specs=[anywhere] * count,
+        scratch_shapes=[pltpu.VMEM(array.shape, array.dtype) for array in arrays]
+        + [pltpu.VMEM(arrays[widened].shape, jnp.float32), pltpu.SemaphoreType.DMA((2, count))],
+        compiler_params=pltpu.CompilerParams(vmem_limit_bytes=62 * 1024 * 1024),
+        name="store",
+    )(*arrays)
+
+
+def wave_matrices(rows):
+    angles = np.pi * ((2 * np.arange(rows)[:, None] + 1) * np.arange(rows)[None, :] % (4 * rows))
+    angles = angles / (2.0 * rows)
+    waves = np.concatenate([np.cos(angles), np.sin(angles)], axis=0).astype(jnp.bfloat16)
+    return (jnp.asarray(waves), jnp.asarray(np.ascontiguousarray(waves.T)))
+
+
+def feature_table(total):
+    places = np.arange(total)
+    frequency = np.arange(1, (EMB - 1) // 2 + 1)
+    angles = 2.0 * np.pi * (places[:, None] * frequency[None, :] % total) / total
+    scaled = places[:, None] / total
+    table = np.concatenate([scaled, np.cos(angles), np.sin(angles)], axis=1).astype(np.float32)
+    table = np.pad(table, ((0, 0), (0, FEATURE_ROWS - EMB)))
+    high = table.astype(jnp.bfloat16)
+    low = (table - high.astype(np.float32)).astype(jnp.bfloat16)
+    table = np.concatenate([high, low, high], axis=1)
+    return jnp.asarray(table)
+
+
+def local_line(sections, parts, *args):
+    (
+        inputs,
+        cotangent,
+        seq_lengths,
+        decay_rates,
+        norm_gain,
+        norm_bias,
+        in_weight,
+        in_bias,
+        short_weight,
+        short_bias,
+        filter_weight_one,
+        filter_bias_one,
+        filter_weight_two,
+        filter_bias_two,
+        filter_weight_out,
+        filter_bias_out,
+        skip_gain,
+        out_weight,
+        out_bias,
+        second_norm_gain,
+        second_norm_bias,
+        up_weight,
+        up_bias,
+        down_weight,
+        down_bias,
+    ) = args
+    micro, held, share = inputs.shape
+    width, hidden_width = up_weight.shape[1:]
+    group = parts // micro
+    total = parts * held
+    rows = total // group
+    geometry = (sections, parts, group, rows, width, hidden_width)
+    features = feature_table(total)
+    waves, waves_back = wave_matrices(rows)
+    operands = dict(
+        inputs=jnp.swapaxes(inputs, 1, 2),
+        cot=jnp.swapaxes(cotangent, 1, 2),
+        w_in=in_weight[0],
+        w_out=out_weight[0],
+        w_up=up_weight[0],
+        w_down=down_weight[0],
+        lengths=seq_lengths,
+        features=features,
+        waves_back=waves_back,
+        decay=decay_rates,
+        filter_one=jnp.swapaxes(filter_weight_one, 0, 1),
+        filter_one_bias=filter_bias_one,
+        filter_two=filter_weight_two[0],
+        filter_two_bias=filter_bias_two,
+        filter_out=filter_weight_out[0],
+        filter_out_bias=filter_bias_out,
+        waves=waves,
+        norm_gain=norm_gain,
+        norm_bias=norm_bias,
+        in_bias=in_bias,
+        short_weight=jnp.swapaxes(short_weight, 0, 1),
+        short_bias=short_bias,
+        skip_gain=skip_gain,
+        out_bias=out_bias,
+        second_norm_gain=second_norm_gain,
+        second_norm_bias=second_norm_bias,
+        up_bias=up_bias,
+        down_bias=down_bias,
+    )
+    made = chain_call(geometry, operands)
+    names = list(vars(made))[:-8]
+    stored = store_call([getattr(made, name) for name in names])
+    sums = types.SimpleNamespace(**dict(zip(names, stored)))
+    return (
+        jnp.swapaxes(sums.outputs, 1, 2),
+        jnp.swapaxes(sums.input_grad, 1, 2),
+        sums.norm_gain_grad,
+        sums.norm_bias_grad,
+        sums.in_grad[None],
+        sums.in_bias_grad,
+        jnp.swapaxes(sums.short_weight_grad, 0, 1),
+        sums.short_bias_grad,
+        sums.filter_one_grad.T[None],
+        sums.filter_one_bias_grad,
+        sums.filter_two_grad[None],
+        sums.filter_two_bias_grad,
+        sums.filter_out_grad[None],
+        sums.filter_out_bias_grad,
+        sums.skip_gain_grad,
+        sums.out_grad[None],
+        sums.out_bias_grad,
+        sums.second_gain_grad,
+        sums.second_bias_grad,
+        sums.up_grad[None],
+        sums.up_bias_grad,
+        sums.down_grad[None],
+        sums.down_bias_grad,
+    )
+
+
+def fits_line(mesh, inputs, up_weight):
+    sections, parts = mesh.shape["section"], mesh.shape["dp"]
+    micro, tokens, width = inputs.shape
+    return (
+        parts == 4 * micro
+        and tokens == 1024
+        and width == 6 * LANES
+        and up_weight.shape[2] == 4 * width
+        and width % sections == 0
+        and sections > 1
+    )
+
+
 def solution(mesh):
     in_specs = (
         P(None, "dp", "section"),
@@ -590,4 +2300,14 @@
         P("section", "dp", None),
         P("section", "dp"),
     )
-    return jax.shard_map(local, mesh=mesh, in_specs=in_specs, out_specs=out_specs, check_vma=False)
+
+    def whole(*args):
+        if fits_line(mesh, args[0], args[21]):
+            body = functools.partial(local_line, mesh.shape["section"], mesh.shape["dp"])
+        else:
+            body = local_general
+        return jax.shard_map(
+            body, mesh=mesh, in_specs=in_specs, out_specs=out_specs, check_vma=False
+        )(*args)
+
+    return whole

time: 2100 us -> 256 us (0.12)
  waiting for transfers between devices: 972 us -> 0 us
  matrix products: 393 us -> 0 us
  starting transfers between devices: 283 us -> 0 us
  Pallas kernels: 0 us -> 254 us
  local copies, waits for them, and re-layouts: 196 us -> 0 us
  other arithmetic: 172 us -> 0 us
  loops' own time: 30.7 us -> 0 us
    all_to_all x66 -> x0, waiting for transfers between devices: 491 us -> none  [the longest x11 99.8 us: forward_transform(): lax.all_to_all(as_sent(real_twist), 'dp', split_axis=0, concat_axis=1, ti...]
    dot_general x200 -> x0, matrix products: 393 us -> none  [the longest x132 141 us: exact_einsum(): return jnp.einsum(pattern, former, latter, precision=highest)]
    reduce_scatter x7 -> x0, waiting for transfers between devices: 392 us -> none  [the longest x1 101 us: local(): lax.psum_scatter(all_grads[17], 'dp', scatter_dimension=0, tiled=True)]
    pallas_call x0 -> x2, Pallas kernels: none -> 254 us  [the longest x1 250 us: chain_call(): pl.pallas_call(functools.partial(chain_kernel, geometry, names), out_shap...]
    all_to_all x66 -> x0, starting transfers between devices: 243 us -> none  [the longest x11 46 us: forward_transform(): lax.all_to_all(signal.reshape(part_count, block_rows, -1).astype(jnp.bflo...]
    unnamed x11 -> x0, waiting for transfers between devices: 79.2 us -> none
    reduce_sum x56 -> x0, other arithmetic: 59.3 us -> none  [the longest x25 25.7 us: layer_norm(): centred = signal - jnp.mean(signal, axis=-1, keepdims=True)]
    convert_element_type x55 -> x0, local copies, waits for them, and re-layouts: 55.4 us -> none  [as_sent(): a.astype(jnp.bfloat16)]
  transfers between devices with their start and end apart: 95 -> 0, of which waited for: 84 -> 0; matrix products, arithmetic and copies ran while one was open for 16% -> 0% of each run, Pallas kernels for 0% -> 0%
where the time goes in v1:
time: 256 us; the launch traced here: 255 us
  Pallas kernels  254 us (99%)
    pallas_call x1, Pallas kernels, chain_call(): pl.pallas_call(functools.partial(chain_kernel, geometry, names), out_shap...  250 us

profile of v1, /device:TPU:0, one launch (start us, length us, event | category | flops | bytes accessed | tf_op | source)
XLA Modules:
  0.0 254.7 jit_solution(16597103609838640908)
XLA Ops:
  0.7 249.9 %chain.1 = (bf16[2,192,128]{2,1,0:T(8,128)(2,1)}, bf16[2,192,128]{2,1,0:T(8,128)(2,1)}, f32[1,96]{1,0:T(1,128)}, f32[1,96]{1,0:T(1,128)}, f32[96,2304]{1,0:T(8,1...) custom-call(bf16[2,192,128]{2,1,0:T(8,128)(2,1)} %bitcast.27, ...), custom_call_target="tpu_custom_call" | custom-call | tf_op jit(solution)/shard_map/chain/pallas_call | solution.py:2069
  250.6 3.9 %store.1 = (bf16[2,192,128]{2,1,0:T(8,128)(2,1)}, f32[2,192,128]{2,1,0:T(8,128)}, f32[1,96]{1,0:T(1,128)}, f32[1,96]{1,0:T(1,128)}, f32[96,2304]{1,0:T(8,128)}, ...) custom-call(bf16[2,192,128]{2,1,0:T(8,128)(2,1)} %get-tuple-element., ...), custom_call_target="tpu_custom_call" | custom-call | tf_op jit(solution)/shard_map/store/pallas_call | solution.py:2106
